TPU v7x, 32 devices: a whole 2x2x4 slice. The times are simulated.
32 devices in a mesh: dp: 4 (over z), ctx: 2 (over y), tp: 4 (over x, core).
Axes of the slice: x: 2, y: 2, z: 4, core: 2. Of those that a mesh axis runs over, the one named last changes fastest.
Arguments:
- q_feat: bfloat16 [2048, 4096], P(('dp', 'ctx'), 'tp'), parts along dimension 0, may hold values from -6 to 6
- k_feat: bfloat16 [2048, 4096], P(('dp', 'ctx'), 'tp'), parts along dimension 0, may hold values from -6 to 6
- v_feat: bfloat16 [2048, 4096], P(('dp', 'ctx'), 'tp'), parts along dimension 0, may hold values from -6 to 6
- short_taps: float32 [3, 3, 4096], P(None, None, 'tp'), may hold values from -3 to 3
- decay_rate: float32 [4096, 16], P('tp'), may hold values from 0.000390625 to 0.04
- residue: float32 [4096, 16], P('tp'), may hold values from -4 to 4
- out_weight: bfloat16 [4096, 4096], P('tp', 'ctx'), may hold values from -0.8125 to 0.8125
- direction: float32 [4096], replicated, may hold values from -120 to 120
Outputs:
- ablated: bfloat16 [2048, 4096], P(('dp', 'ctx'), 'tp'), parts along dimension 0
- feature_level: float32 [2048], P(('dp', 'ctx')), parts along dimension 0
There are 4 independent parts, one for each index of `dp`. A program takes and returns all parts, laid end to end along the dimension named above; an argument that names none is the same for every part. Nothing has to cross between parts.
All inputs are finite; a program needn't handle non-finite values.
Results may differ from a plain program's by a relative error of at most 0.019.
Values may be sent and summed in bfloat16 or wider, within the bound.
No kernel may reach another device: no remote copies, remote signals or barrier semaphores. Data moves between devices by JAX's collectives and lax.ppermute only.
A program may use at most 128 MiB of HBM per device.

v0:
```python
import functools

import jax
import jax.numpy as jnp
from jax import lax
from jax.experimental import pallas as pl
from jax.experimental.pallas import tpu as pltpu
from jax.sharding import PartitionSpec as P

EPSILON = 1e-06
HIGHEST = lax.Precision.HIGHEST
LANES = 128
GROUP = 8
STEP = 16
WHOLE = pl.BlockSpec(memory_space=pltpu.VMEM)
AWAY = pl.BlockSpec(memory_space=pltpu.HBM)


def params(mebibytes=20):
    return pltpu.CompilerParams(vmem_limit_bytes=mebibytes * 1024 * 1024)


def cost(flops):
    return pl.CostEstimate(flops=flops, bytes_accessed=1024, transcendentals=0)


def spread(source, scratch, row, to):
    blocks = source.shape[1] // LANES
    for block in range(blocks):
        piece = source[pl.ds(row, STEP), block * LANES : (block + 1) * LANES].astype(jnp.float32)
        for half in range(STEP // GROUP):
            start = (half * blocks + block) * GROUP
            scratch[pl.ds(to + start, GROUP), :] = piece[half * GROUP : (half + 1) * GROUP]


def spread_rows(source, target):
    count, width = source.shape
    blocks = width // LANES
    for block in range(blocks):
        target[pl.ds(block, count, stride=blocks), :] = source[:, block * LANES : (block + 1) * LANES]


def place_of(index, blocks):
    return pl.ds((index // GROUP) * (blocks * GROUP) + index % GROUP, blocks, stride=GROUP)


def tile(ref, index, blocks):
    return ref[index * blocks : (index + 1) * blocks, :]


def moving_tile(index, blocks):
    return pl.ds(pl.multiple_of(index * blocks, blocks), blocks)


def front_kernel(*refs):
    k_hbm, v_hbm, q_hbm, taps_hbm, rate_hbm, residue_hbm = refs[:6]
    carry_ref, signal_ref, decay_ref, taps_ref, edge_ref, rate_ref, residue_ref, q_near = refs[6:14]
    k_near, v_near, taps_near, *wides, sems, late_sems = refs[-9:]
    wides = (wides[:2], wides[2:])
    rows, width = k_near.shape
    blocks = width // LANES
    modes = rate_ref.shape[0]
    pieces = sems.shape[0] // 2 - 1
    height = rows // pieces

    def part(i):
        here = pl.ds(i * height, height)
        return (
            pltpu.make_async_copy(k_hbm.at[here], k_near.at[here], sems.at[2 * i]),
            pltpu.make_async_copy(v_hbm.at[here], v_near.at[here], sems.at[2 * i + 1]),
        )

    rate_copy = pltpu.make_async_copy(rate_hbm, rate_ref, sems.at[2 * pieces])
    taps_copy = pltpu.make_async_copy(taps_hbm, taps_near, sems.at[2 * pieces + 1])
    late = [(residue_hbm, residue_ref), (q_hbm, q_near)]
    late = [pltpu.make_async_copy(source, target, late_sems.at[i]) for i, (source, target) in enumerate(late)]
    rate_copy.start()
    taps_copy.start()
    for i in range(pieces):
        for copy in part(i):
            copy.start()
    for copy in late:
        copy.start()
    rate_copy.wait()
    taps_copy.wait()
    spread_rows(jnp.exp(-rate_ref[...]), decay_ref)
    for i in range(3):
        for block in range(blocks):
            taps_ref[pl.ds(3 * i * blocks + block, 3, stride=blocks), :] = taps_near[
                i, :, block * LANES : (block + 1) * LANES
            ]
    zero = jnp.zeros((blocks, LANES), jnp.float32)
    key_taps = [tile(taps_ref, 3 + j, blocks) for j in range(3)]
    value_taps = [tile(taps_ref, 6 + j, blocks) for j in range(3)]
    decay = [tile(decay_ref, m, blocks) for m in range(modes)]

    def step(row, held):
        state, (k2, k1, v2, v1) = list(held[:modes]), held[modes:]
        for half, (k_wide, v_wide) in enumerate(wides):
            spread(k_near, k_wide, row + half * STEP, 0)
            spread(v_near, v_wide, row + half * STEP, 0)
        for half, (k_wide, v_wide) in enumerate(wides):
            for index in range(STEP):
                k0 = k_wide[place_of(index, blocks), :]
                v0 = v_wide[place_of(index, blocks), :]
                key = key_taps[0] * k0 + key_taps[1] * k1 + key_taps[2] * k2
                value = value_taps[0] * v0 + value_taps[1] * v1 + value_taps[2] * v2
                signal = key * value
                signal_ref[moving_tile(row + half * STEP + index, blocks), :] = signal
                state = [decay[m] * state[m] + signal for m in range(modes)]
                k2, k1, v2, v1 = k1, k0, v1, v0
        return tuple(state) + (k2, k1, v2, v1)

    held = (zero,) * (modes + 4)
    for i in range(pieces):
        for copy in part(i):
            copy.wait()
        if i == 0:
            spread(k_near, wides[0][0], 0, 0)
            spread(v_near, wides[0][1], 0, 0)
            for wide, taps, place in ((wides[0][0], key_taps, 0), (wides[0][1], value_taps, 2)):
                x0, x1 = wide[place_of(0, blocks), :], wide[place_of(1, blocks), :]
                edge_ref[place * blocks : (place + 1) * blocks, :] = taps[0] * x0
                edge_ref[(place + 1) * blocks : (place + 2) * blocks, :] = taps[0] * x1 + taps[1] * x0
        held = lax.fori_loop(
            0,
            height // (2 * STEP),
            lambda j, held, i=i: step(pl.multiple_of(i * height + j * 2 * STEP, 2 * STEP), held),
            held,
        )
    for m in range(modes + 4):
        carry_ref[m * blocks : (m + 1) * blocks, :] = held[m]
    for copy in late:
        copy.wait()
    k_wide = wides[0][0]
    spread(q_near, k_wide, rows - STEP, 0)
    for i in range(2):
        start = (modes + 4 + i) * blocks
        carry_ref[start : start + blocks, :] = k_wide[place_of(STEP - 2 + i, blocks), :]


def far(x):
    return pltpu.with_memory_space_constraint(x, pltpu.HBM)


def run_front(q, k, v, short_taps, rate, residue):
    rows, width = k.shape
    modes = rate.shape[0]
    blocks = width // LANES
    pieces = 4

    def wide(n):
        return jax.ShapeDtypeStruct((n * blocks, LANES), jnp.float32)

    def like(x):
        return jax.ShapeDtypeStruct(x.shape, x.dtype)

    out_shape = [wide(modes + 6), wide(rows), wide(modes), wide(9), wide(4), like(rate), like(residue), like(q)]
    return pl.pallas_call(
        front_kernel,
        out_shape=out_shape,
        in_specs=[AWAY] * 6,
        out_specs=[WHOLE] * len(out_shape),
        scratch_shapes=[
            pltpu.VMEM((rows, width), jnp.bfloat16),
            pltpu.VMEM((rows, width), jnp.bfloat16),
            pltpu.VMEM(short_taps.shape, jnp.float32),
            *[pltpu.VMEM((STEP * blocks, LANES), jnp.float32)] * 4,
            pltpu.SemaphoreType.DMA((2 * pieces + 2,)),
            pltpu.SemaphoreType.DMA((2,)),
        ],
        compiler_params=params(),
        cost_estimate=cost(10**8),
        name="front",
    )(*[far(x) for x in (k, v, q, short_taps, rate, residue)])


def local_kernel(q_near, signal_ref, decay_ref, taps_ref, gain_near, *refs):
    copies = []
    if len(refs) > 5:
        weight_hbm, direction_hbm, weight_ref, direction_ref, sems = refs[:2] + refs[5:7] + refs[-1:]
        refs = refs[2:5] + refs[7:-1]
        count = sems.shape[0] - 1
        copies.append(pltpu.make_async_copy(direction_hbm, direction_ref, sems.at[count]))
        copies[-1].start()
        depth = weight_ref.shape[0] // count
        for i in range(count):
            here = pl.ds(i * depth, depth)
            copies.append(pltpu.make_async_copy(weight_hbm.at[here], weight_ref.at[here], sems.at[i]))
            copies[-1].start()
    out_ref, query_ref, gain_ref, *wides = refs
    rows, width = q_near.shape
    blocks = width // LANES
    modes = gain_near.shape[0]
    spread_rows(gain_near[...], gain_ref)
    zero = jnp.zeros((blocks, LANES), jnp.float32)
    taps = [tile(taps_ref, j, blocks) for j in range(3)]
    decay = [tile(decay_ref, m, blocks) for m in range(modes)]
    gain = [tile(gain_ref, m, blocks) for m in range(modes)]

    def step(j, held):
        row = pl.multiple_of(j * 2 * STEP, 2 * STEP)
        state, (q2, q1) = list(held[:modes]), held[modes:]
        for half, q_wide in enumerate(wides):
            spread(q_near, q_wide, row + half * STEP, 0)
        for half, q_wide in enumerate(wides):
            for index in range(STEP):
                q0 = q_wide[place_of(index, blocks), :]
                here = moving_tile(row + half * STEP + index, blocks)
                signal = signal_ref[here, :]
                query_ref[here, :] = taps[0] * q0 + taps[1] * q1 + taps[2] * q2
                state = [decay[m] * state[m] + signal for m in range(modes)]
                sums = [gain[m] * state[m] for m in range(modes)]
                while len(sums) > 1:
                    sums = [sums[i] + sums[i + 1] for i in range(0, len(sums), 2)]
                out_ref[here, :] = sums[0]
                q2, q1 = q1, q0
        return tuple(state) + (q2, q1)

    lax.fori_loop(0, rows // (2 * STEP), step, (zero,) * (modes + 2))
    for copy in copies:
        copy.wait()


def run_local(q, signal, decay, taps, gain, *weight):
    rows, width = q.shape
    blocks = width // LANES
    wide = jax.ShapeDtypeStruct((rows * blocks, LANES), jnp.float32)
    out_shape = [wide, wide, jax.ShapeDtypeStruct(decay.shape, jnp.float32)]
    scratch_shapes = [pltpu.VMEM((STEP * blocks, LANES), jnp.float32)] * 2
    if weight:
        out_shape += [jax.ShapeDtypeStruct(x.shape, x.dtype) for x in weight]
        scratch_shapes.append(pltpu.SemaphoreType.DMA((5,)))
        weight = tuple(far(x) for x in weight)
    return pl.pallas_call(
        local_kernel,
        out_shape=out_shape,
        in_specs=[WHOLE] * 5 + [AWAY] * len(weight),
        out_specs=[WHOLE] * len(out_shape),
        scratch_shapes=scratch_shapes,
        compiler_params=params(),
        cost_estimate=cost(10**6),
        name="local_filter",
    )(q, signal, decay, taps, gain, *weight)


def correct_kernel(blocks, start, decay_ref, gain_ref, local_ref, query_ref, *refs):
    out_ref, state_out_ref, wide = refs[-3:]
    rows = out_ref.shape[0]
    modes = decay_ref.shape[0] // blocks
    decay = [tile(decay_ref, m, blocks) for m in range(modes)]
    extra = query_extra = ()
    if start:
        state = tuple(tile(refs[0], m, blocks) for m in range(modes))
    else:
        carry_ref, taps_ref, edge_ref = refs[:3]
        carried = jnp.where(lax.axis_index("ctx") > 0, 1.0, 0.0)
        k2, k1, v2, v1, q2, q1 = [carried * tile(carry_ref, modes + i, blocks) for i in range(6)]
        tap = [tile(taps_ref, i, blocks) for i in range(9)]
        key0, key1, value0, value1 = [tile(edge_ref, i, blocks) for i in range(4)]
        extra = (
            (key0 + tap[4] * k1 + tap[5] * k2) * (value0 + tap[7] * v1 + tap[8] * v2) - key0 * value0,
            (key1 + tap[5] * k1) * (value1 + tap[8] * v1) - key1 * value1,
        )
        query_extra = (tap[1] * q1 + tap[2] * q2, tap[2] * q1)
        state = tuple(tile(gain_ref, m, blocks) * (carried * tile(carry_ref, m, blocks)) for m in range(modes))

    def step(row, state, first):
        state = list(state)
        for index in range(STEP):
            here = moving_tile(start + row + index, blocks)
            state = [decay[m] * state[m] for m in range(modes)]
            query = query_ref[here, :]
            if first and index < 2:
                state = [state[m] + tile(gain_ref, m, blocks) * extra[index] for m in range(modes)]
                query = query + query_extra[index]
            sums = state
            while len(sums) > 1:
                sums = [sums[i] + sums[i + 1] for i in range(0, len(sums), 2)]
            wide[place_of(index, blocks), :] = query * (local_ref[here, :] + sums[0])
        for block in range(blocks):
            halves = [
                wide[(half * blocks + block) * GROUP : (half * blocks + block + 1) * GROUP, :]
                for half in range(STEP // GROUP)
            ]
            out_ref[pl.ds(row, STEP), block * LANES : (block + 1) * LANES] = jnp.concatenate(
                halves, axis=0
            ).astype(jnp.bfloat16)
        return tuple(state)

    begin = 0
    if start == 0:
        state = step(0, state, True)
        begin = 1
    state = lax.fori_loop(
        begin, rows // STEP, lambda j, state: step(pl.multiple_of(j * STEP, STEP), state, False), state
    )
    for m in range(modes):
        state_out_ref[m * blocks : (m + 1) * blocks, :] = state[m]


def run_correct(start, rows, decay, gain, local, query, blocks, *before):
    return pl.pallas_call(
        functools.partial(correct_kernel, blocks, start),
        out_shape=[
            jax.ShapeDtypeStruct((rows, blocks * LANES), jnp.bfloat16),
            jax.ShapeDtypeStruct(decay.shape, jnp.float32),
        ],
        in_specs=[WHOLE] * (4 + len(before)),
        out_specs=[WHOLE] * 2,
        scratch_shapes=[pltpu.VMEM((STEP * blocks, LANES), jnp.float32)],
        compiler_params=params(),
        cost_estimate=cost(10**8),
        name="carried_filter",
    )(decay, gain, local, query, *before)


def gains_of(rate, residue):
    return residue * jnp.sqrt(-jnp.expm1(-2.0 * rate)) * rate.shape[0] ** (-0.5)


def split_three(x):
    high = x.astype(jnp.bfloat16)
    rest = x - high.astype(jnp.float32)
    middle = rest.astype(jnp.bfloat16)
    low = (rest - middle.astype(jnp.float32)).astype(jnp.bfloat16)
    return high, middle, low


def in_parts(row):
    return jnp.concatenate(list(split_three(row)) + [jnp.zeros((13, row.shape[1]), jnp.bfloat16)], axis=0)


def dot_parts(parts, matrix):
    out = lax.dot_general(parts, matrix, (((1,), (1,)), ((), ())), preferred_element_type=jnp.float32)
    return out[0:1] + out[1:2] + out[2:3]


def idle_kernel(*refs):
    pass


def after(array, *others):
    return pl.pallas_call(
        idle_kernel,
        out_shape=jax.ShapeDtypeStruct(array.shape, array.dtype),
        in_specs=[pl.BlockSpec(memory_space=pl.ANY)] * (1 + len(others)),
        out_specs=pl.BlockSpec(memory_space=pl.ANY),
        input_output_aliases={0: 0},
        compiler_params=params(),
        cost_estimate=cost(1),
        name="after",
    )(array, *others)


def rows_of(count, like, dtype=jnp.bfloat16):
    return jax.ShapeDtypeStruct((count, like.shape[1]), dtype)


def call(kernel, name, out_shape, *operands, tokens=()):
    def with_tokens(*refs):
        kernel(*refs[: len(operands)], *refs[len(operands) + len(tokens) :])

    return pl.pallas_call(
        with_tokens,
        out_shape=out_shape,
        in_specs=[WHOLE] * len(operands) + [pl.BlockSpec(memory_space=pl.ANY)] * len(tokens),
        out_specs=[WHOLE] * len(out_shape),
        compiler_params=params(),
        cost_estimate=cost(10**6),
        name=name,
    )(*operands, *tokens)


def inner_kernel(direction_ref, weight_ref, parts_ref, norm_ref, here_ref):
    everything = direction_ref[...]
    norm_ref[...] = jnp.broadcast_to(
        jnp.sum(everything * everything, axis=1, keepdims=True) + EPSILON, norm_ref.shape
    )
    size, width = weight_ref.shape[1], here_ref.shape[1]
    here_ref[...] = direction_ref[:, pl.ds(pl.multiple_of(lax.axis_index("tp") * width, LANES), width)]
    here = direction_ref[:, pl.ds(pl.multiple_of(lax.axis_index("ctx") * size, LANES), size)]
    parts_ref[...] = in_parts(dot_parts(in_parts(here), weight_ref[...]))


def run_inner(direction, weight):
    out_shape = [
        jax.ShapeDtypeStruct((STEP, weight.shape[0]), jnp.bfloat16),
        jax.ShapeDtypeStruct((1, LANES), jnp.float32),
        jax.ShapeDtypeStruct((1, weight.shape[1] // 2), jnp.float32),
    ]
    return call(inner_kernel, "inner", out_shape, direction, weight)


def project_kernel(begin, rows, away, weight_ref, piece_ref, *outs):
    cut = outs[0].shape[1]
    width = cut * len(outs)
    side = lax.axis_index("tp") % 2
    which = 1 - side if away else side
    for start in range(0, width, 256):
        columns = pl.ds(pl.multiple_of(which * width + start, 256), 256)
        out = jnp.dot(piece_ref[begin : begin + rows, :], weight_ref[:, columns], preferred_element_type=jnp.float32)
        ref, to = outs[start // cut], start % cut
        ref[:, to : to + 256] = out.astype(ref.dtype)


def run_project(weight, piece, begin, rows, count, *tokens):
    width = weight.shape[1] // 2
    sends = [jax.ShapeDtypeStruct((rows, width // count), jnp.bfloat16)] * count
    keep = [jax.ShapeDtypeStruct((rows, width), jnp.float32)]
    away, here = [functools.partial(project_kernel, begin, rows, x) for x in (True, False)]
    sends = call(away, "project", sends, weight, piece, tokens=tokens)
    return sends, call(here, "project", keep, weight, piece, tokens=tokens)[0]


def put_behind(ref, rows, row):
    here = slice(rows, rows + STEP)
    ref[here, :] = jnp.zeros((STEP, ref.shape[1]), jnp.bfloat16)
    ref[here, : row.shape[1]] = in_parts(row)


def take_behind(ref, rows, width):
    return jnp.sum(ref[rows : rows + STEP, :width].astype(jnp.float32), axis=0, keepdims=True)


def level_kernel(parts_ref, far_ref, *refs):
    *pieces, out_ref = refs
    far_parts = far_ref[far_ref.shape[0] - STEP :, :]
    start = 0
    for piece in pieces:
        end = start + piece.shape[0]
        out_ref[:, start:end] = dot_parts(parts_ref[...], piece[...]) + dot_parts(far_parts, piece[...])
        start = end


def add_shares(lefts, rights, outs):
    width = sum(ref.shape[1] for ref in lefts)
    rows = lefts[0].shape[0]
    step = min(ref.shape[1] for ref in (*lefts, *rights, *outs))

    def at(pieces, row, column):
        size = pieces[0].shape[1]
        return pieces[column // size].at[row : row + STEP, column % size : column % size + step]

    for row in range(0, rows, STEP):
        for column in range(0, width, step):
            left = at(lefts, row, column)[...].astype(jnp.float32)
            right = at(rights, row, column)[...].astype(jnp.float32)
            at(outs, row, column)[...] = (left + right).astype(jnp.bfloat16)


def merge_kernel(left, right, *refs):
    add_shares(refs[:left], refs[left : left + right], refs[left + right :])


def run_merge(lefts, rights, count):
    rows, width = lefts[0].shape[0], sum(x.shape[1] for x in lefts)
    kernel = functools.partial(merge_kernel, len(lefts), len(rights))
    out_shape = [jax.ShapeDtypeStruct((rows, width // count), jnp.bfloat16)] * count
    return call(kernel, "merge", out_shape, *lefts, *rights)


def merge_parts_kernel(keep_ref, parts_ref, *refs):
    add_shares((keep_ref,), refs[:-1], refs[-1:])
    refs[-1][keep_ref.shape[0] :, :] = parts_ref[...]


def is_keeper():
    return lax.axis_index("tp") // 2 == lax.axis_index("ctx")


def choose_kernel(straight_ref, own_ref, level_ref, other_ref, out_ref, total_ref):
    keeper = is_keeper()

    @pl.when(keeper)
    def _():
        rows = straight_ref.shape[0] - STEP
        out_ref[:rows, :] = straight_ref[:rows, :]

    @pl.when(jnp.logical_not(keeper))
    def _():
        out_ref[: own_ref.shape[0], :] = own_ref[...]

    total = level_ref[...] + other_ref[...]
    total_ref[...] = total
    put_behind(out_ref, out_ref.shape[0] - STEP, total)


def finish_kernel(*refs):
    level_ref, norm_ref, direction_ref = refs[:3]
    own0, own1, (straight_ref, merged_ref) = refs[3:6], refs[6:9], refs[9:11]
    out_hbm, level_hbm, out_near, level_near, sems = refs[11:]
    turned_ref = own1[-1]
    rows, width = out_near.shape
    half = straight_ref.shape[0] - STEP
    keeper = is_keeper()
    level = (level_ref[...] + take_behind(turned_ref, turned_ref.shape[0] - STEP, rows)) / norm_ref[0:1, 0:1]
    level_near[...] = level
    copies = [pltpu.make_async_copy(level_near, level_hbm, sems.at[sems.shape[0] - 1])]
    copies[0].start()
    direction = direction_ref[...]
    column = jnp.transpose(jnp.broadcast_to(level, (LANES, rows)))

    def put(row, cut, before, behind):
        pieces, start = (before, row) if row < cut else (behind, row - cut)
        total = pieces[0][start : start + STEP, :].astype(jnp.float32)
        for piece in pieces[1:]:
            total = total + piece[start : start + STEP, :].astype(jnp.float32)
        total = total - column[row : row + STEP, 0:1] * direction
        out_near[row : row + STEP, :] = total.astype(jnp.bfloat16)

    count = sems.shape[0] - 1
    for i in range(count):
        begin, end = i * rows // count, (i + 1) * rows // count

        @pl.when(keeper)
        def _():
            for row in range(begin, end, STEP):
                put(row, own0[0].shape[0], own0, own1)

        @pl.when(jnp.logical_not(keeper))
        def _():
            for row in range(begin, end, STEP):
                put(row, half, (straight_ref, turned_ref), (merged_ref,))

        here = pl.ds(begin, end - begin)
        copies.append(pltpu.make_async_copy(out_near.at[here], out_hbm.at[here], sems.at[i]))
        copies[-1].start()
    for copy in copies:
        copy.wait()


def run_finish(*operands):
    rows, width = operands[0].shape[1], operands[2].shape[1]
    return pl.pallas_call(
        finish_kernel,
        out_shape=[pltpu.HBM((rows, width), jnp.bfloat16), pltpu.HBM((1, rows), jnp.float32)],
        in_specs=[WHOLE] * len(operands),
        out_specs=[AWAY] * 2,
        scratch_shapes=[
            pltpu.VMEM((rows, width), jnp.bfloat16),
            pltpu.VMEM((1, rows), jnp.float32),
            pltpu.SemaphoreType.DMA((5,)),
        ],
        compiler_params=params(),
        cost_estimate=cost(10**6),
        name="finish",
    )(*operands)


def plane_plan(q, k, v, short_taps, decay_rate, residue, out_weight, direction):
    rows, width = q.shape
    cut = rows // 2
    blocks = width // LANES
    axes = ("ctx", "tp")
    across = [(4 * c + p, 4 * (1 - c) + p) for c in range(2) for p in range(4)]
    sibling = [(4 * c + p, 4 * c + (p ^ 1)) for c in range(2) for p in range(4)]
    pair = [(4 * c + p, 4 * c + (p ^ 2)) for c in range(2) for p in range(4)]

    ended, signal, decay, taps, edge, rate, residue, q = run_front(q, k, v, short_taps, decay_rate.T, residue.T)
    carry = lax.ppermute(ended, axes, across)
    local, query, gain, weight, direction = run_local(
        q, signal, decay, taps, gains_of(rate, residue), out_weight, direction.reshape(1, -1)
    )
    first, state = run_correct(0, cut, decay, gain, local, query, blocks, carry, taps, edge)
    second, _ = run_correct(cut, rows - cut, decay, gain, local, query, blocks, state)
    far_first = lax.ppermute(first, axes, across)
    far_second = lax.ppermute(second, axes, across)

    def exchange(arrays, pairs):
        return [lax.ppermute(array, axes, pairs) for array in arrays]

    weight = after(weight, first)
    parts, norm, direction = run_inner(direction, weight)
    sends0, keep0 = run_project(weight, first, 0, cut, 1)
    sends1, keep1 = run_project(weight, second, 0, rows - cut, 1)
    (core0,) = exchange(sends0, sibling)
    (hop0,) = exchange(run_merge((keep0,), (core0,), 1), pair)

    sends, far_keep = run_project(weight, far_first, 0, cut, 2, parts, *sends0, *sends1)
    (sums0,) = call(
        merge_parts_kernel, "merge", [rows_of(cut + STEP, far_keep)], far_keep, parts, *exchange(sends, sibling)
    )
    (straight,) = exchange([sums0], across)

    sends, far_keep = run_project(weight, after(far_second, sums0, hop0), 0, rows - cut, 2)
    sums1 = run_merge((far_keep,), exchange(sends, sibling), 2)
    moved = exchange(sums1, pair)
    (core1,) = exchange(sends1, sibling)
    (own1,) = run_merge((keep1,), (core1,), 1)

    one_row = jax.ShapeDtypeStruct((1, rows), jnp.float32)
    (level,) = call(level_kernel, "level", [one_row], parts, straight, first, second)
    payload = rows_of(max(cut, rows - cut) + STEP, far_keep)
    turned, level = call(
        choose_kernel,
        "choose",
        [payload, one_row],
        straight,
        own1,
        level,
        *exchange([level], sibling),
    )
    (turned,) = exchange([turned], pair)
    (merged,) = exchange(run_merge(sums1, moved, 1), across)
    ablated, level = run_finish(
        level, norm, direction, keep0, core0, hop0, keep1, core1, turned, straight, merged
    )
    return ablated, level.reshape(rows)


def gather_plan(q, k, v, short_taps, decay_rate, residue, out_weight, direction):
    rows, width = q.shape
    blocks = width // LANES
    modes = decay_rate.shape[1]
    tp = lax.axis_index("tp")
    ctx_size = lax.axis_size("ctx")
    next_one = [(i, i + 1) for i in range(ctx_size - 1)]
    ended, signal, decay, taps, edge, rate, residue, q = run_front(q, k, v, short_taps, decay_rate.T, residue.T)
    halo = lax.ppermute(ended[modes * blocks :], "ctx", next_one)
    local, query, gain = run_local(q, signal, decay, taps, gains_of(rate, residue))
    k2, k1, v2, v1 = [halo[i * blocks : (i + 1) * blocks] for i in range(4)]
    tap = taps.reshape(9, blocks, LANES)
    key0, key1, value0, value1 = edge.reshape(4, blocks, LANES)
    extra0 = (key0 + tap[4] * k1 + tap[5] * k2) * (value0 + tap[7] * v1 + tap[8] * v2) - key0 * value0
    extra1 = (key1 + tap[5] * k1) * (value1 + tap[8] * v1) - key1 * value1
    wide_rate = decay_rate.T.reshape(modes, blocks, LANES)
    state = (
        ended[: modes * blocks].reshape(modes, blocks, LANES)
        + jnp.exp(-wide_rate * (rows - 1)) * extra0
        + jnp.exp(-wide_rate * (rows - 2)) * extra1
    )
    reach = 1
    while reach < ctx_size:
        earlier = lax.ppermute(state, "ctx", [(i, i + reach) for i in range(ctx_size - reach)])
        state = state + jnp.exp(-wide_rate * (rows * reach)) * earlier
        reach *= 2
    start = lax.ppermute(state, "ctx", next_one).reshape(modes * blocks, LANES)
    carry = jnp.concatenate([start, halo], axis=0)
    gated, _ = run_correct(0, rows, decay, gain, local, query, blocks, carry, taps, edge)
    partial_terms = lax.dot_general(
        gated,
        lax.all_gather(out_weight, "ctx", axis=1, tiled=True),
        (((1,), (0,)), ((), ())),
        preferred_element_type=jnp.float32,
    )
    summed = lax.psum_scatter(
        partial_terms.astype(jnp.bfloat16), "tp", scatter_dimension=1, tiled=True
    ).astype(jnp.float32)
    width_here = summed.shape[1]
    direction_here = lax.dynamic_slice_in_dim(direction, tp * width_here, width_here, 0)
    norm_total = jnp.sum(direction * direction) + EPSILON
    local_inner = jnp.dot(summed, direction_here, precision=HIGHEST)
    feature_level = lax.psum(local_inner, "tp") / norm_total
    ablated = (summed - feature_level[:, None] * direction_here[None, :]).astype(jnp.bfloat16)
    return ablated, feature_level


def solution(mesh):
    placed = (
        P(("dp", "ctx"), "tp"),
        P(("dp", "ctx"), "tp"),
        P(("dp", "ctx"), "tp"),
        P(None, None, "tp"),
        P("tp", None),
        P("tp", None),
        P("tp", "ctx"),
        P(),
    )
    plane = mesh.shape["ctx"] == 2 and mesh.shape["tp"] == 4
    return jax.shard_map(
        plane_plan if plane else gather_plan,
        mesh=mesh,
        in_specs=placed,
        out_specs=(P(("dp", "ctx"), "tp"), P(("dp", "ctx"))),
        check_vma=False,
    )
```

profile of v0, /device:TPU:0, one launch (start us, length us, event | category | flops | bytes accessed | tf_op | source)
XLA Modules:
  0.0 45.1 jit_solution(10643272268227106605)
XLA Ops:
  0.6 2.9 %front.1 = (f32[176,128]{1,0:T(8,128)S(1)}, f32[2048,128]{1,0:T(8,128)S(1)}, f32[128,128]{1,0:T(8,128)S(1)}, f32[72,128]{1,0:T(8,128)S(1)}, f32[32,128]{1,0:T(8,...) custom-call(bf16[256,1024]{1,0:T(8,128)(2,1)} %refs_0_.2, ...), custom_call_target="tpu_custom_call" | custom-call | flops 100000000 | bytes 1024 | tf_op jit(solution)/shard_map/front/pallas_call | solution.py:159
  3.6 3.0 %collective-permute-start = (f32[176,128]{1,0:T(8,128)S(1)}, f32[176,128]{1,0:T(8,128)S(1)}, u32[]{:S(2)}, u32[]{:S(2)}) collective-permute-start(f32[176,128]{1,0:T(8,128)S(1)} %get-tuple-element.41), channel_id=1, source_target_pairs={{0,4},{1,5},{2,6},{3,7},{4,0},{5,1},{6,2},{7,3},{8,12},{9,13},{10,... | collective-permute-start | bytes 270344 | tf_op jit(solution)/shard_map/ppermute | solution.py:561
  6.7 2.9 %local_filter.1 = (f32[2048,128]{1,0:T(8,128)S(1)}, f32[2048,128]{1,0:T(8,128)S(1)}, f32[128,128]{1,0:T(8,128)S(1)}, bf16[1024,2048]{1,0:T(8,128)(2,1)S(1)}, f32[1,4096]{1,0:T(1,128)S(1)}) custom-call(bf16[256,1024]{1,0:T(8,128)(2,1)S(1)} %get-tuple-element.31.q_near, f32[2048,128]{1,0:T(8,128)S(1)} %get-tuple-element.32.signal_ref, ...), custom_call_target="tpu_custom_call" | custom-call | flops 1000000 | bytes 1024 | tf_op jit(solution)/shard_map/local_filter/pallas_call | solution.py:235
  9.6 0.7 %carried_filter.2 = (bf16[128,1024]{1,0:T(8,128)(2,1)S(1)}, f32[128,128]{1,0:T(8,128)S(1)}) custom-call(f32[128,128]{1,0:T(8,128)S(1)} %get-tuple-element.33.decay_ref, f32[128,128]{1,0:T(8,128)S(1)} %get-tuple-element.38.gain_ref, f32[2048,128]{1,0:T(8,128)S(1)} %get-tuple-element.39.local_ref, f32[2048,128]{1,0:T(8,128)S(1)} %get-tuple-element.40.query_ref, ...), custom_call_target="tpu_custom_call" | custom-call | flops 100000000 | bytes 1024 | tf_op jit(solution)/shard_map/carried_filter/pallas_call | solution.py:303
  10.9 1.6 %collective-permute-start.1 = (bf16[128,1024]{1,0:T(8,128)(2,1)S(1)}, bf16[128,1024]{1,0:T(8,128)(2,1)S(1)}, u32[]{:S(2)}, u32[]{:S(2)}) collective-permute-start(bf16[128,1024]{1,0:T(8,128)(2,1)S(1)} %get-tuple-element.43.refs_1_.refs_2_), channel_id=1, source_target_pairs={{0,4},{1,5},{2,6},{3,7},{4,0},{5,1},{6,2},{7,3},{8,12},{9,13},{10,... | collective-permute-start | bytes 786440 | tf_op jit(solution)/shard_map/ppermute | solution.py:567
  12.5 1.3 %carried_filter.3 = (bf16[128,1024]{1,0:T(8,128)(2,1)S(1)}, f32[128,128]{1,0:T(8,128)}) custom-call(f32[128,128]{1,0:T(8,128)S(1)} %get-tuple-element.33.decay_ref, f32[128,128]{1,0:T(8,128)S(1)} %get-tuple-element.38.gain_ref, f32[2048,128]{1,0:T(8,128)S(1)} %get-tuple-element.39.local_ref, f32[2048,128]{1,0:T(8,128)S(1)} %get-tuple-element.40.query_ref, ...), custom_call_target="tpu_custom_call" | custom-call | flops 100000000 | bytes 1024 | tf_op jit(solution)/shard_map/carried_filter/pallas_call | solution.py:303
  13.8 0.5 %collective-permute-start.10 = (bf16[128,1024]{1,0:T(8,128)(2,1)S(1)}, bf16[128,1024]{1,0:T(8,128)(2,1)S(1)}, u32[]{:S(2)}, u32[]{:S(2)}) collective-permute-start(bf16[128,1024]{1,0:T(8,128)(2,1)S(1)} %get-tuple-element.47.refs_1_.refs_3_), channel_id=1, source_target_pairs={{0,4},{1,5},{2,6},{3,7},{4,0},{5,1},{6,2},{7,3},{8,12},{9,13},{10,... | collective-permute-start | bytes 786440 | tf_op jit(solution)/shard_map/ppermute | solution.py:568
  14.9 1.6 %collective-permute-start.8 = (bf16[128,1024]{1,0:T(8,128)(2,1)S(1)}, bf16[128,1024]{1,0:T(8,128)(2,1)S(1)}, u32[]{:S(2)}, u32[]{:S(2)}) collective-permute-start(bf16[128,1024]{1,0:T(8,128)(2,1)S(1)} %merge.7), channel_id=1, source_target_pairs={{0,2},{1,3},{2,0},{3,1},{4,6},{5,7},{6,4},{7,5},{8,10},{9,11},{10,... | collective-permute-start | bytes 786440 | tf_op jit(solution)/shard_map/ppermute | solution.py:571
  16.9 1.2 %inner.1 = (bf16[16,1024]{1,0:T(8,128)(2,1)S(1)}, f32[1,128]{1,0:T(1,128)S(1)}, f32[1,1024]{1,0:T(1,128)S(1)}) custom-call(f32[1,4096]{1,0:T(1,128)S(1)} %get-tuple-element.44.refs_0_, bf16[1024,2048]{1,0:T(8,128)(2,1)S(1)} %after.2.refs_1_.refs_0_), custom_call_target="tpu_custom_call" | custom-call | flops 1000000 | bytes 1024 | tf_op jit(solution)/shard_map/inner/pallas_call | solution.py:364
  18.1 1.9 %collective-permute-done.1.refs_1_ = bf16[128,1024]{1,0:T(8,128)(2,1)S(1)} collective-permute-done((bf16[128,1024]{1,0:T(8,128)(2,1)S(1)}, bf16[128,1024]{1,0:T(8,128)(2,1)S(1)}, u32[]{:S(2)}, u32[]{:S(2)}) %collective-permute-start.1) | collective-permute-done | bytes 262176 | tf_op jit(solution)/shard_map/ppermute | solution.py:567
  20.6 0.5 %collective-permute-start.3 = (bf16[128,512]{1,0:T(8,128)(2,1)S(1)}, bf16[128,512]{1,0:T(8,128)(2,1)S(1)}, u32[]{:S(2)}, u32[]{:S(2)}) collective-permute-start(bf16[128,512]{1,0:T(8,128)(2,1)S(1)} %get-tuple-element.49), channel_id=1, source_target_pairs={{0,1},{1,0},{2,3},{3,2},{4,5},{5,4},{6,7},{7,6},{8,9},{9,8},{10,11... | collective-permute-start | bytes 393224 | tf_op jit(solution)/shard_map/ppermute | solution.py:571
  22.2 1.6 %collective-permute-start.4 = (bf16[144,1024]{1,0:T(8,128)(2,1)S(1)}, bf16[144,1024]{1,0:T(8,128)(2,1)S(1)}, u32[]{:S(2)}, u32[]{:S(2)}) collective-permute-start(bf16[144,1024]{1,0:T(8,128)(2,1)S(1)} %merge.5.refs_1_), channel_id=1, source_target_pairs={{0,4},{1,5},{2,6},{3,7},{4,0},{5,1},{6,2},{7,3},{8,12},{9,13},{10,... | collective-permute-start | bytes 884744 | tf_op jit(solution)/shard_map/ppermute | solution.py:571
  23.8 1.4 %collective-permute-done.10.refs_0_ = bf16[128,1024]{1,0:T(8,128)(2,1)S(1)} collective-permute-done((bf16[128,1024]{1,0:T(8,128)(2,1)S(1)}, bf16[128,1024]{1,0:T(8,128)(2,1)S(1)}, u32[]{:S(2)}, u32[]{:S(2)}) %collective-permute-start.10) | collective-permute-done | bytes 262176 | tf_op jit(solution)/shard_map/ppermute | solution.py:568
  27.4 1.6 %collective-permute-start.13 = (bf16[128,512]{1,0:T(8,128)(2,1)S(1)}, bf16[128,512]{1,0:T(8,128)(2,1)S(1)}, u32[]{:S(2)}, u32[]{:S(2)}) collective-permute-start(bf16[128,512]{1,0:T(8,128)(2,1)S(1)} %get-tuple-element.56.refs_0_), channel_id=1, source_target_pairs={{0,2},{1,3},{2,0},{3,1},{4,6},{5,7},{6,4},{7,5},{8,10},{9,11},{10,... | collective-permute-start | bytes 393224 | tf_op jit(solution)/shard_map/ppermute | solution.py:571
  28.9 0.5 %collective-permute-start.14 = (bf16[128,512]{1,0:T(8,128)(2,1)S(1)}, bf16[128,512]{1,0:T(8,128)(2,1)S(1)}, u32[]{:S(2)}, u32[]{:S(2)}) collective-permute-start(bf16[128,512]{1,0:T(8,128)(2,1)S(1)} %get-tuple-element.57.refs_1_), channel_id=1, source_target_pairs={{0,2},{1,3},{2,0},{3,1},{4,6},{5,7},{6,4},{7,5},{8,10},{9,11},{10,... | collective-permute-start | bytes 393224 | tf_op jit(solution)/shard_map/ppermute | solution.py:571
  29.5 2.1 %collective-permute-done.4.refs_1_.refs_0_.refs_9_ = bf16[144,1024]{1,0:T(8,128)(2,1)S(1)} collective-permute-done((bf16[144,1024]{1,0:T(8,128)(2,1)S(1)}, bf16[144,1024]{1,0:T(8,128)(2,1)S(1)}, u32[]{:S(2)}, u32[]{:S(2)}) %collective-permute-start.4) | collective-permute-done | bytes 294944 | tf_op jit(solution)/shard_map/ppermute | solution.py:571
  31.9 0.5 %project.12.refs_0_.refs_6_ = f32[128,1024]{1,0:T(8,128)S(1)} custom-call(bf16[1024,2048]{1,0:T(8,128)(2,1)S(1)} %after.2.refs_1_.refs_0_, bf16[128,1024]{1,0:T(8,128)(2,1)S(1)} %get-tuple-element.47.refs_1_.refs_3_), custom_call_target="tpu_custom_call" | custom-call | flops 1000000 | bytes 1024 | tf_op jit(solution)/shard_map/project/pallas_call | solution.py:364
  32.5 0.6 %collective-permute-done.6.refs_3_ = f32[1,256]{1,0:T(1,128)S(1)} collective-permute-done((f32[1,256]{1,0:T(1,128)S(1)}, f32[1,256]{1,0:T(1,128)S(1)}, u32[]{:S(2)}, u32[]{:S(2)}) %collective-permute-start.6) | collective-permute-done | bytes 1056 | tf_op jit(solution)/shard_map/ppermute | solution.py:571
  33.1 1.6 %collective-permute-start.9 = (bf16[144,1024]{1,0:T(8,128)(2,1)S(1)}, bf16[144,1024]{1,0:T(8,128)(2,1)S(1)}, u32[]{:S(2)}, u32[]{:S(2)}) collective-permute-start(bf16[144,1024]{1,0:T(8,128)(2,1)S(1)} %get-tuple-element.53), channel_id=1, source_target_pairs={{0,2},{1,3},{2,0},{3,1},{4,6},{5,7},{6,4},{7,5},{8,10},{9,11},{10,... | collective-permute-start | bytes 884744 | tf_op jit(solution)/shard_map/ppermute | solution.py:571
  34.7 1.3 %collective-permute-done.14.refs_3_ = bf16[128,512]{1,0:T(8,128)(2,1)S(1)} collective-permute-done((bf16[128,512]{1,0:T(8,128)(2,1)S(1)}, bf16[128,512]{1,0:T(8,128)(2,1)S(1)}, u32[]{:S(2)}, u32[]{:S(2)}) %collective-permute-start.14) | collective-permute-done | bytes 131104 | tf_op jit(solution)/shard_map/ppermute | solution.py:571
  36.0 1.6 %collective-permute-start.15 = (bf16[128,1024]{1,0:T(8,128)(2,1)S(1)}, bf16[128,1024]{1,0:T(8,128)(2,1)S(1)}, u32[]{:S(2)}, u32[]{:S(2)}) collective-permute-start(bf16[128,1024]{1,0:T(8,128)(2,1)S(1)} %merge.9), channel_id=1, source_target_pairs={{0,4},{1,5},{2,6},{3,7},{4,0},{5,1},{6,2},{7,3},{8,12},{9,13},{10,... | collective-permute-start | bytes 786440 | tf_op jit(solution)/shard_map/ppermute | solution.py:571
  37.6 4.7 %collective-permute-done.9.refs_8_ = bf16[144,1024]{1,0:T(8,128)(2,1)S(1)} collective-permute-done((bf16[144,1024]{1,0:T(8,128)(2,1)S(1)}, bf16[144,1024]{1,0:T(8,128)(2,1)S(1)}, u32[]{:S(2)}, u32[]{:S(2)}) %collective-permute-start.9) | collective-permute-done | bytes 294944 | tf_op jit(solution)/shard_map/ppermute | solution.py:571
  42.3 1.5 %collective-permute-done.15.refs_10_ = bf16[128,1024]{1,0:T(8,128)(2,1)S(1)} collective-permute-done((bf16[128,1024]{1,0:T(8,128)(2,1)S(1)}, bf16[128,1024]{1,0:T(8,128)(2,1)S(1)}, u32[]{:S(2)}, u32[]{:S(2)}) %collective-permute-start.15) | collective-permute-done | bytes 262176 | tf_op jit(solution)/shard_map/ppermute | solution.py:571
  43.8 1.3 %finish.1 = (bf16[256,1024]{1,0:T(8,128)(2,1)}, f32[1,256]{1,0:T(1,128)}) custom-call(f32[1,256]{1,0:T(1,128)S(1)} %get-tuple-element.50.refs_0_, f32[1,128]{1,0:T(1,128)S(1)} %get-tuple-element.51.refs_1_, f32[1,1024]{1,0:T(1,128)S(1)} %get-tuple-element.52.refs_2_, f32[128,1024]{1,0:T(8,128)S(1)} %project.13.refs_0_.refs_3_, ...), custom_call_target="tpu_custom_call" | custom-call | flops 1000000 | bytes 1024 | tf_op jit(solution)/shard_map/finish/pallas_call | solution.py:535
  (32 shorter events, 5.9 us)
Async XLA Ops:
  3.6 6.0 %collective-permute-start = (f32[176,128]{1,0:T(8,128)S(1)}, f32[176,128]{1,0:T(8,128)S(1)}, u32[]{:S(2)}, u32[]{:S(2)}) collective-permute-start(f32[176,128]{1,0:T(8,128)S(1)} %get-tuple-element.41), channel_id=1, source_target_pairs={{0,4},{1,5},{2,6},{3,7},{4,0},{5,1},{6,2},{7,3},{8,12},{9,13},{10,... | collective-permute-start | bytes 270344 | tf_op jit(solution)/shard_map/ppermute | solution.py:561
  10.8 4.0 %collective-permute-start.7 = (bf16[128,1024]{1,0:T(8,128)(2,1)S(1)}, bf16[128,1024]{1,0:T(8,128)(2,1)S(1)}, u32[]{:S(2)}, u32[]{:S(2)}) collective-permute-start(bf16[128,1024]{1,0:T(8,128)(2,1)S(1)} %project.8.refs_3_), channel_id=1, source_target_pairs={{0,1},{1,0},{2,3},{3,2},{4,5},{5,4},{6,7},{7,6},{8,9},{9,8},{10,11... | collective-permute-start | bytes 786440 | tf_op jit(solution)/shard_map/ppermute | solution.py:571
  10.9 9.2 %collective-permute-start.1 = (bf16[128,1024]{1,0:T(8,128)(2,1)S(1)}, bf16[128,1024]{1,0:T(8,128)(2,1)S(1)}, u32[]{:S(2)}, u32[]{:S(2)}) collective-permute-start(bf16[128,1024]{1,0:T(8,128)(2,1)S(1)} %get-tuple-element.43.refs_1_.refs_2_), channel_id=1, source_target_pairs={{0,4},{1,5},{2,6},{3,7},{4,0},{5,1},{6,2},{7,3},{8,12},{9,13},{10,... | collective-permute-start | bytes 786440 | tf_op jit(solution)/shard_map/ppermute | solution.py:567
  13.8 11.4 %collective-permute-start.10 = (bf16[128,1024]{1,0:T(8,128)(2,1)S(1)}, bf16[128,1024]{1,0:T(8,128)(2,1)S(1)}, u32[]{:S(2)}, u32[]{:S(2)}) collective-permute-start(bf16[128,1024]{1,0:T(8,128)(2,1)S(1)} %get-tuple-element.47.refs_1_.refs_3_), channel_id=1, source_target_pairs={{0,4},{1,5},{2,6},{3,7},{4,0},{5,1},{6,2},{7,3},{8,12},{9,13},{10,... | collective-permute-start | bytes 786440 | tf_op jit(solution)/shard_map/ppermute | solution.py:568
  14.9 10.4 %collective-permute-start.8 = (bf16[128,1024]{1,0:T(8,128)(2,1)S(1)}, bf16[128,1024]{1,0:T(8,128)(2,1)S(1)}, u32[]{:S(2)}, u32[]{:S(2)}) collective-permute-start(bf16[128,1024]{1,0:T(8,128)(2,1)S(1)} %merge.7), channel_id=1, source_target_pairs={{0,2},{1,3},{2,0},{3,1},{4,6},{5,7},{6,4},{7,5},{8,10},{9,11},{10,... | collective-permute-start | bytes 786440 | tf_op jit(solution)/shard_map/ppermute | solution.py:571
  20.6 1.4 %collective-permute-start.2 = (bf16[128,512]{1,0:T(8,128)(2,1)S(1)}, bf16[128,512]{1,0:T(8,128)(2,1)S(1)}, u32[]{:S(2)}, u32[]{:S(2)}) collective-permute-start(bf16[128,512]{1,0:T(8,128)(2,1)S(1)} %get-tuple-element.48), channel_id=1, source_target_pairs={{0,1},{1,0},{2,3},{3,2},{4,5},{5,4},{6,7},{7,6},{8,9},{9,8},{10,11... | collective-permute-start | bytes 393224 | tf_op jit(solution)/shard_map/ppermute | solution.py:571
  20.6 1.5 %collective-permute-start.3 = (bf16[128,512]{1,0:T(8,128)(2,1)S(1)}, bf16[128,512]{1,0:T(8,128)(2,1)S(1)}, u32[]{:S(2)}, u32[]{:S(2)}) collective-permute-start(bf16[128,512]{1,0:T(8,128)(2,1)S(1)} %get-tuple-element.49), channel_id=1, source_target_pairs={{0,1},{1,0},{2,3},{3,2},{4,5},{5,4},{6,7},{7,6},{8,9},{9,8},{10,11... | collective-permute-start | bytes 393224 | tf_op jit(solution)/shard_map/ppermute | solution.py:571
  22.2 9.4 %collective-permute-start.4 = (bf16[144,1024]{1,0:T(8,128)(2,1)S(1)}, bf16[144,1024]{1,0:T(8,128)(2,1)S(1)}, u32[]{:S(2)}, u32[]{:S(2)}) collective-permute-start(bf16[144,1024]{1,0:T(8,128)(2,1)S(1)} %merge.5.refs_1_), channel_id=1, source_target_pairs={{0,4},{1,5},{2,6},{3,7},{4,0},{5,1},{6,2},{7,3},{8,12},{9,13},{10,... | collective-permute-start | bytes 884744 | tf_op jit(solution)/shard_map/ppermute | solution.py:571
  23.8 8.6 %collective-permute-start.5 = (bf16[128,1024]{1,0:T(8,128)(2,1)S(1)}, bf16[128,1024]{1,0:T(8,128)(2,1)S(1)}, u32[]{:S(2)}, u32[]{:S(2)}) collective-permute-start(bf16[128,1024]{1,0:T(8,128)(2,1)S(1)} %project.9.refs_4_), channel_id=1, source_target_pairs={{0,1},{1,0},{2,3},{3,2},{4,5},{5,4},{6,7},{7,6},{8,9},{9,8},{10,11... | collective-permute-start | bytes 786440 | tf_op jit(solution)/shard_map/ppermute | solution.py:571
  25.7 1.4 %collective-permute-start.11 = (bf16[128,512]{1,0:T(8,128)(2,1)S(1)}, bf16[128,512]{1,0:T(8,128)(2,1)S(1)}, u32[]{:S(2)}, u32[]{:S(2)}) collective-permute-start(bf16[128,512]{1,0:T(8,128)(2,1)S(1)} %get-tuple-element.54), channel_id=1, source_target_pairs={{0,1},{1,0},{2,3},{3,2},{4,5},{5,4},{6,7},{7,6},{8,9},{9,8},{10,11... | collective-permute-start | bytes 393224 | tf_op jit(solution)/shard_map/ppermute | solution.py:571
  25.8 1.5 %collective-permute-start.12 = (bf16[128,512]{1,0:T(8,128)(2,1)S(1)}, bf16[128,512]{1,0:T(8,128)(2,1)S(1)}, u32[]{:S(2)}, u32[]{:S(2)}) collective-permute-start(bf16[128,512]{1,0:T(8,128)(2,1)S(1)} %get-tuple-element.55), channel_id=1, source_target_pairs={{0,1},{1,0},{2,3},{3,2},{4,5},{5,4},{6,7},{7,6},{8,9},{9,8},{10,11... | collective-permute-start | bytes 393224 | tf_op jit(solution)/shard_map/ppermute | solution.py:571
  27.4 7.3 %collective-permute-start.13 = (bf16[128,512]{1,0:T(8,128)(2,1)S(1)}, bf16[128,512]{1,0:T(8,128)(2,1)S(1)}, u32[]{:S(2)}, u32[]{:S(2)}) collective-permute-start(bf16[128,512]{1,0:T(8,128)(2,1)S(1)} %get-tuple-element.56.refs_0_), channel_id=1, source_target_pairs={{0,2},{1,3},{2,0},{3,1},{4,6},{5,7},{6,4},{7,5},{8,10},{9,11},{10,... | collective-permute-start | bytes 393224 | tf_op jit(solution)/shard_map/ppermute | solution.py:571
  28.9 7.0 %collective-permute-start.14 = (bf16[128,512]{1,0:T(8,128)(2,1)S(1)}, bf16[128,512]{1,0:T(8,128)(2,1)S(1)}, u32[]{:S(2)}, u32[]{:S(2)}) collective-permute-start(bf16[128,512]{1,0:T(8,128)(2,1)S(1)} %get-tuple-element.57.refs_1_), channel_id=1, source_target_pairs={{0,2},{1,3},{2,0},{3,1},{4,6},{5,7},{6,4},{7,5},{8,10},{9,11},{10,... | collective-permute-start | bytes 393224 | tf_op jit(solution)/shard_map/ppermute | solution.py:571
  31.9 1.2 %collective-permute-start.6 = (f32[1,256]{1,0:T(1,128)S(1)}, f32[1,256]{1,0:T(1,128)S(1)}, u32[]{:S(2)}, u32[]{:S(2)}) collective-permute-start(f32[1,256]{1,0:T(1,128)S(1)} %level.1.refs_2_), channel_id=1, source_target_pairs={{0,1},{1,0},{2,3},{3,2},{4,5},{5,4},{6,7},{7,6},{8,9},{9,8},{10,11... | collective-permute-start | bytes 3080 | tf_op jit(solution)/shard_map/ppermute | solution.py:571
  33.1 9.2 %collective-permute-start.9 = (bf16[144,1024]{1,0:T(8,128)(2,1)S(1)}, bf16[144,1024]{1,0:T(8,128)(2,1)S(1)}, u32[]{:S(2)}, u32[]{:S(2)}) collective-permute-start(bf16[144,1024]{1,0:T(8,128)(2,1)S(1)} %get-tuple-element.53), channel_id=1, source_target_pairs={{0,2},{1,3},{2,0},{3,1},{4,6},{5,7},{6,4},{7,5},{8,10},{9,11},{10,... | collective-permute-start | bytes 884744 | tf_op jit(solution)/shard_map/ppermute | solution.py:571
  36.0 7.8 %collective-permute-start.15 = (bf16[128,1024]{1,0:T(8,128)(2,1)S(1)}, bf16[128,1024]{1,0:T(8,128)(2,1)S(1)}, u32[]{:S(2)}, u32[]{:S(2)}) collective-permute-start(bf16[128,1024]{1,0:T(8,128)(2,1)S(1)} %merge.9), channel_id=1, source_target_pairs={{0,4},{1,5},{2,6},{3,7},{4,0},{5,1},{6,2},{7,3},{8,12},{9,13},{10,... | collective-permute-start | bytes 786440 | tf_op jit(solution)/shard_map/ppermute | solution.py:571
where the time goes:
time: 45.2 us; the launch traced here: 45.1 us
  Pallas kernels  14.9 us (33%)
  starting transfers between devices  14.8 us (33%)
  waiting for transfers between devices  14.6 us (32%)
  between operations  0.81 us (2%)
    ppermute x13, waiting for transfers between devices, exchange(): return [lax.ppermute(array, axes, pairs) for array in arrays]  11.3 us
    ppermute x13, starting transfers between devices, exchange(): return [lax.ppermute(array, axes, pairs) for array in arrays]  9.66 us
    pallas_call x16, Pallas kernels, call(): pl.pallas_call(with_tokens, out_shape=out_shape, in_specs=[WHOLE] * len(o...  5.72 us
    ppermute x1, starting transfers between devices, plane_plan(): carry = lax.ppermute(ended, axes, across)  3.03 us
    pallas_call x1, Pallas kernels, run_front(): pl.pallas_call(front_kernel, out_shape=out_shape, in_specs=[AWAY] * 6, ou...  2.93 us
    pallas_call x1, Pallas kernels, run_local(): pl.pallas_call(local_kernel, out_shape=out_shape, in_specs=[WHOLE] * 5 +...  2.92 us
    pallas_call x2, Pallas kernels, run_correct(): pl.pallas_call(functools.partial(correct_kernel, blocks, start), out_shap...  2.04 us
    ppermute x1, waiting for transfers between devices, plane_plan(): far_first = lax.ppermute(first, axes, across)  1.93 us
  transfers between devices with their start and end apart: 16, of which 11 were waited for; matrix products, arithmetic and copies ran while one was open for 0% of the time, Pallas kernels for 21%

commit v1 on v0

--- a/solution.py
+++ b/solution.py
@@ -486,66 +486,74 @@
     put_behind(out_ref, out_ref.shape[0] - STEP, total)
 
 
-def finish_kernel(*refs):
-    level_ref, norm_ref, direction_ref = refs[:3]
-    own0, own1, (straight_ref, merged_ref) = refs[3:6], refs[6:9], refs[9:11]
-    out_hbm, level_hbm, out_near, level_near, sems = refs[11:]
-    turned_ref = own1[-1]
-    rows, width = out_near.shape
-    half = straight_ref.shape[0] - STEP
+def finish_kernel(start, count, *refs):
+    level_ref, norm_ref, direction_ref, keep_ref, core_ref, hop_ref, first_ref = refs[:7]
+    second_ref = None if start else refs[7]
+    rows = level_ref.shape[1]
+    if start:
+        out_hbm, out_near, sems = refs[-3:]
+        level = level_ref[...]
+        copies = []
+    else:
+        out_hbm, level_hbm, level_near, level_out, out_near, sems = refs[-6:]
+        level = level_ref[...] + take_behind(second_ref, second_ref.shape[0] - STEP, rows)
+        level = level / norm_ref[0:1, 0:1]
+        level_near[...] = level
+        level_out[...] = level
+        copies = [pltpu.make_async_copy(level_out, level_hbm, sems.at[2])]
+        copies[0].start()
+    direction = direction_ref[...]
     keeper = is_keeper()
-    level = (level_ref[...] + take_behind(turned_ref, turned_ref.shape[0] - STEP, rows)) / norm_ref[0:1, 0:1]
-    level_near[...] = level
-    copies = [pltpu.make_async_copy(level_near, level_hbm, sems.at[sems.shape[0] - 1])]
-    copies[0].start()
-    direction = direction_ref[...]
     column = jnp.transpose(jnp.broadcast_to(level, (LANES, rows)))
 
-    def put(row, cut, before, behind):
-        pieces, start = (before, row) if row < cut else (behind, row - cut)
-        total = pieces[0][start : start + STEP, :].astype(jnp.float32)
+    def put(row, *pieces):
+        here = slice(row, row + STEP)
+        total = pieces[0][here, :].astype(jnp.float32)
         for piece in pieces[1:]:
-            total = total + piece[start : start + STEP, :].astype(jnp.float32)
-        total = total - column[row : row + STEP, 0:1] * direction
-        out_near[row : row + STEP, :] = total.astype(jnp.bfloat16)
-
-    count = sems.shape[0] - 1
-    for i in range(count):
-        begin, end = i * rows // count, (i + 1) * rows // count
+            total = total + piece[here, :].astype(jnp.float32)
+        total = total - column[start + row : start + row + STEP, 0:1] * direction
+        out_near[here, :] = total.astype(jnp.bfloat16)
+
+    for i in range(2):
+        begin, end = i * count // 2, (i + 1) * count // 2
 
         @pl.when(keeper)
         def _():
             for row in range(begin, end, STEP):
-                put(row, own0[0].shape[0], own0, own1)
+                put(row, keep_ref, core_ref, hop_ref)
 
         @pl.when(jnp.logical_not(keeper))
         def _():
             for row in range(begin, end, STEP):
-                put(row, half, (straight_ref, turned_ref), (merged_ref,))
-
-        here = pl.ds(begin, end - begin)
-        copies.append(pltpu.make_async_copy(out_near.at[here], out_hbm.at[here], sems.at[i]))
+                put(row, *((first_ref,) if start else (first_ref, second_ref)))
+
+        here, there = pl.ds(begin, end - begin), pl.ds(start + begin, end - begin)
+        copies.append(pltpu.make_async_copy(out_near.at[here], out_hbm.at[there], sems.at[i]))
         copies[-1].start()
     for copy in copies:
         copy.wait()
 
 
-def run_finish(*operands):
-    rows, width = operands[0].shape[1], operands[2].shape[1]
+def run_finish(start, rows, operands, before=()):
+    count, width = operands[3].shape
+    one_row = jax.ShapeDtypeStruct((1, rows), jnp.float32)
+    out_shape, out_specs = [pltpu.HBM((rows, width), jnp.bfloat16)], [AWAY]
+    scratch_shapes = [pltpu.VMEM((count, width), jnp.bfloat16), pltpu.SemaphoreType.DMA((3,))]
+    if not before:
+        out_shape += [pltpu.HBM(one_row.shape, one_row.dtype), one_row]
+        out_specs += [AWAY, WHOLE]
+        scratch_shapes = [pltpu.VMEM(one_row.shape, one_row.dtype)] + scratch_shapes
     return pl.pallas_call(
-        finish_kernel,
-        out_shape=[pltpu.HBM((rows, width), jnp.bfloat16), pltpu.HBM((1, rows), jnp.float32)],
-        in_specs=[WHOLE] * len(operands),
-        out_specs=[AWAY] * 2,
-        scratch_shapes=[
-            pltpu.VMEM((rows, width), jnp.bfloat16),
-            pltpu.VMEM((1, rows), jnp.float32),
-            pltpu.SemaphoreType.DMA((5,)),
-        ],
+        functools.partial(finish_kernel, start, count),
+        out_shape=out_shape,
+        in_specs=[WHOLE] * len(operands) + [AWAY] * len(before),
+        out_specs=out_specs,
+        scratch_shapes=scratch_shapes,
+        input_output_aliases={len(operands): 0} if before else {},
         compiler_params=params(),
         cost_estimate=cost(10**6),
         name="finish",
-    )(*operands)
+    )(*operands, *[far(x) for x in before])
 
 
 def plane_plan(q, k, v, short_taps, decay_rate, residue, out_weight, direction):
@@ -603,9 +611,9 @@
     )
     (turned,) = exchange([turned], pair)
     (merged,) = exchange(run_merge(sums1, moved, 1), across)
-    ablated, level = run_finish(
-        level, norm, direction, keep0, core0, hop0, keep1, core1, turned, straight, merged
-    )
+    shared = (norm, direction)
+    before, level, near = run_finish(0, rows, (level, *shared, keep0, core0, hop0, straight, turned))
+    (ablated,) = run_finish(cut, rows, (near, *shared, keep1, core1, turned, merged), (before,))
     return ablated, level.reshape(rows)
 
 

time: 45.2 us -> 45 us (level)
  waiting for transfers between devices: 14.6 us -> 13.5 us
  Pallas kernels: 14.9 us -> 15.6 us
    ppermute x13, waiting for transfers between devices: 11.3 us -> 10.2 us  [exchange(): return [lax.ppermute(array, axes, pairs) for array in arrays]]
    pallas_call x1 -> x2, Pallas kernels: 1.25 us -> 2.02 us  [run_finish(): pl.pallas_call(functools.partial(finish_kernel, start, count), out_shape=...]
  transfers between devices with their start and end apart: 16 -> 16, of which waited for: 11 -> 11; matrix products, arithmetic and copies ran while one was open for 0% -> 0% of each run, Pallas kernels for 21% -> 23%
where the time goes in v1:
time: 45 us; the launch traced here: 44.8 us
  Pallas kernels  15.6 us (35%)
  starting transfers between devices  14.8 us (33%)
  waiting for transfers between devices  13.5 us (30%)
  between operations  0.82 us (2%)
    ppermute x13, waiting for transfers between devices, exchange(): return [lax.ppermute(array, axes, pairs) for array in arrays]  10.2 us
    ppermute x13, starting transfers between devices, exchange(): return [lax.ppermute(array, axes, pairs) for array in arrays]  9.65 us
    pallas_call x16, Pallas kernels, call(): pl.pallas_call(with_tokens, out_shape=out_shape, in_specs=[WHOLE] * len(o...  5.72 us
    ppermute x1, starting transfers between devices, plane_plan(): carry = lax.ppermute(ended, axes, across)  3.03 us
    pallas_call x1, Pallas kernels, run_front(): pl.pallas_call(front_kernel, out_shape=out_shape, in_specs=[AWAY] * 6, ou...  2.93 us
    pallas_call x1, Pallas kernels, run_local(): pl.pallas_call(local_kernel, out_shape=out_shape, in_specs=[WHOLE] * 5 +...  2.92 us
    pallas_call x2, Pallas kernels, run_correct(): pl.pallas_call(functools.partial(correct_kernel, blocks, start), out_shap...  2.04 us
    pallas_call x2, Pallas kernels, run_finish(): pl.pallas_call(functools.partial(finish_kernel, start, count), out_shape=...  2.02 us
  transfers between devices with their start and end apart: 16, of which 11 were waited for; matrix products, arithmetic and copies ran while one was open for 0% of the time, Pallas kernels for 23%

profile of v1, /device:TPU:0, one launch (start us, length us, event | category | flops | bytes accessed | tf_op | source)
XLA Modules:
  0.0 44.8 jit_solution(3374741703875851017)
XLA Ops:
  0.6 2.9 %front.1 = (f32[176,128]{1,0:T(8,128)S(1)}, f32[2048,128]{1,0:T(8,128)S(1)}, f32[128,128]{1,0:T(8,128)S(1)}, f32[72,128]{1,0:T(8,128)S(1)}, f32[32,128]{1,0:T(8,...) custom-call(bf16[256,1024]{1,0:T(8,128)(2,1)} %refs_0_.2, ...), custom_call_target="tpu_custom_call" | custom-call | flops 100000000 | bytes 1024 | tf_op jit(solution)/shard_map/front/pallas_call | solution.py:159
  3.6 3.0 %collective-permute-start = (f32[176,128]{1,0:T(8,128)S(1)}, f32[176,128]{1,0:T(8,128)S(1)}, u32[]{:S(2)}, u32[]{:S(2)}) collective-permute-start(f32[176,128]{1,0:T(8,128)S(1)} %get-tuple-element.42), channel_id=1, source_target_pairs={{0,4},{1,5},{2,6},{3,7},{4,0},{5,1},{6,2},{7,3},{8,12},{9,13},{10,... | collective-permute-start | bytes 270344 | tf_op jit(solution)/shard_map/ppermute | solution.py:569
  6.7 2.9 %local_filter.1 = (f32[2048,128]{1,0:T(8,128)S(1)}, f32[2048,128]{1,0:T(8,128)S(1)}, f32[128,128]{1,0:T(8,128)S(1)}, bf16[1024,2048]{1,0:T(8,128)(2,1)S(1)}, f32[1,4096]{1,0:T(1,128)S(1)}) custom-call(bf16[256,1024]{1,0:T(8,128)(2,1)S(1)} %get-tuple-element.32.q_near, f32[2048,128]{1,0:T(8,128)S(1)} %get-tuple-element.33.signal_ref, ...), custom_call_target="tpu_custom_call" | custom-call | flops 1000000 | bytes 1024 | tf_op jit(solution)/shard_map/local_filter/pallas_call | solution.py:235
  9.6 0.7 %carried_filter.2 = (bf16[128,1024]{1,0:T(8,128)(2,1)S(1)}, f32[128,128]{1,0:T(8,128)S(1)}) custom-call(f32[128,128]{1,0:T(8,128)S(1)} %get-tuple-element.34.decay_ref, f32[128,128]{1,0:T(8,128)S(1)} %get-tuple-element.39.gain_ref, f32[2048,128]{1,0:T(8,128)S(1)} %get-tuple-element.40.local_ref, f32[2048,128]{1,0:T(8,128)S(1)} %get-tuple-element.41.query_ref, ...), custom_call_target="tpu_custom_call" | custom-call | flops 100000000 | bytes 1024 | tf_op jit(solution)/shard_map/carried_filter/pallas_call | solution.py:303
  10.9 1.6 %collective-permute-start.1 = (bf16[128,1024]{1,0:T(8,128)(2,1)S(1)}, bf16[128,1024]{1,0:T(8,128)(2,1)S(1)}, u32[]{:S(2)}, u32[]{:S(2)}) collective-permute-start(bf16[128,1024]{1,0:T(8,128)(2,1)S(1)} %get-tuple-element.44.refs_1_.refs_2_), channel_id=1, source_target_pairs={{0,4},{1,5},{2,6},{3,7},{4,0},{5,1},{6,2},{7,3},{8,12},{9,13},{10,... | collective-permute-start | bytes 786440 | tf_op jit(solution)/shard_map/ppermute | solution.py:575
  12.5 1.3 %carried_filter.3 = (bf16[128,1024]{1,0:T(8,128)(2,1)S(1)}, f32[128,128]{1,0:T(8,128)}) custom-call(f32[128,128]{1,0:T(8,128)S(1)} %get-tuple-element.34.decay_ref, f32[128,128]{1,0:T(8,128)S(1)} %get-tuple-element.39.gain_ref, f32[2048,128]{1,0:T(8,128)S(1)} %get-tuple-element.40.local_ref, f32[2048,128]{1,0:T(8,128)S(1)} %get-tuple-element.41.query_ref, ...), custom_call_target="tpu_custom_call" | custom-call | flops 100000000 | bytes 1024 | tf_op jit(solution)/shard_map/carried_filter/pallas_call | solution.py:303
  13.8 0.5 %collective-permute-start.10 = (bf16[128,1024]{1,0:T(8,128)(2,1)S(1)}, bf16[128,1024]{1,0:T(8,128)(2,1)S(1)}, u32[]{:S(2)}, u32[]{:S(2)}) collective-permute-start(bf16[128,1024]{1,0:T(8,128)(2,1)S(1)} %get-tuple-element.48.refs_1_.refs_3_), channel_id=1, source_target_pairs={{0,4},{1,5},{2,6},{3,7},{4,0},{5,1},{6,2},{7,3},{8,12},{9,13},{10,... | collective-permute-start | bytes 786440 | tf_op jit(solution)/shard_map/ppermute | solution.py:576
  14.9 1.6 %collective-permute-start.8 = (bf16[128,1024]{1,0:T(8,128)(2,1)S(1)}, bf16[128,1024]{1,0:T(8,128)(2,1)S(1)}, u32[]{:S(2)}, u32[]{:S(2)}) collective-permute-start(bf16[128,1024]{1,0:T(8,128)(2,1)S(1)} %merge.7), channel_id=1, source_target_pairs={{0,2},{1,3},{2,0},{3,1},{4,6},{5,7},{6,4},{7,5},{8,10},{9,11},{10,... | collective-permute-start | bytes 786440 | tf_op jit(solution)/shard_map/ppermute | solution.py:579
  16.9 1.2 %inner.1 = (bf16[16,1024]{1,0:T(8,128)(2,1)S(1)}, f32[1,128]{1,0:T(1,128)S(1)}, f32[1,1024]{1,0:T(1,128)S(1)}) custom-call(f32[1,4096]{1,0:T(1,128)S(1)} %get-tuple-element.45.refs_0_, bf16[1024,2048]{1,0:T(8,128)(2,1)S(1)} %after.2.refs_1_.refs_0_), custom_call_target="tpu_custom_call" | custom-call | flops 1000000 | bytes 1024 | tf_op jit(solution)/shard_map/inner/pallas_call | solution.py:364
  18.1 1.9 %collective-permute-done.1.refs_1_ = bf16[128,1024]{1,0:T(8,128)(2,1)S(1)} collective-permute-done((bf16[128,1024]{1,0:T(8,128)(2,1)S(1)}, bf16[128,1024]{1,0:T(8,128)(2,1)S(1)}, u32[]{:S(2)}, u32[]{:S(2)}) %collective-permute-start.1) | collective-permute-done | bytes 262176 | tf_op jit(solution)/shard_map/ppermute | solution.py:575
  20.6 0.5 %collective-permute-start.3 = (bf16[128,512]{1,0:T(8,128)(2,1)S(1)}, bf16[128,512]{1,0:T(8,128)(2,1)S(1)}, u32[]{:S(2)}, u32[]{:S(2)}) collective-permute-start(bf16[128,512]{1,0:T(8,128)(2,1)S(1)} %get-tuple-element.50), channel_id=1, source_target_pairs={{0,1},{1,0},{2,3},{3,2},{4,5},{5,4},{6,7},{7,6},{8,9},{9,8},{10,11... | collective-permute-start | bytes 393224 | tf_op jit(solution)/shard_map/ppermute | solution.py:579
  22.2 1.6 %collective-permute-start.4 = (bf16[144,1024]{1,0:T(8,128)(2,1)S(1)}, bf16[144,1024]{1,0:T(8,128)(2,1)S(1)}, u32[]{:S(2)}, u32[]{:S(2)}) collective-permute-start(bf16[144,1024]{1,0:T(8,128)(2,1)S(1)} %merge.5.refs_1_), channel_id=1, source_target_pairs={{0,4},{1,5},{2,6},{3,7},{4,0},{5,1},{6,2},{7,3},{8,12},{9,13},{10,... | collective-permute-start | bytes 884744 | tf_op jit(solution)/shard_map/ppermute | solution.py:579
  23.8 1.4 %collective-permute-done.10.refs_0_ = bf16[128,1024]{1,0:T(8,128)(2,1)S(1)} collective-permute-done((bf16[128,1024]{1,0:T(8,128)(2,1)S(1)}, bf16[128,1024]{1,0:T(8,128)(2,1)S(1)}, u32[]{:S(2)}, u32[]{:S(2)}) %collective-permute-start.10) | collective-permute-done | bytes 262176 | tf_op jit(solution)/shard_map/ppermute | solution.py:576
  27.4 1.6 %collective-permute-start.13 = (bf16[128,512]{1,0:T(8,128)(2,1)S(1)}, bf16[128,512]{1,0:T(8,128)(2,1)S(1)}, u32[]{:S(2)}, u32[]{:S(2)}) collective-permute-start(bf16[128,512]{1,0:T(8,128)(2,1)S(1)} %get-tuple-element.58.refs_0_), channel_id=1, source_target_pairs={{0,2},{1,3},{2,0},{3,1},{4,6},{5,7},{6,4},{7,5},{8,10},{9,11},{10,... | collective-permute-start | bytes 393224 | tf_op jit(solution)/shard_map/ppermute | solution.py:579
  28.9 0.5 %collective-permute-start.14 = (bf16[128,512]{1,0:T(8,128)(2,1)S(1)}, bf16[128,512]{1,0:T(8,128)(2,1)S(1)}, u32[]{:S(2)}, u32[]{:S(2)}) collective-permute-start(bf16[128,512]{1,0:T(8,128)(2,1)S(1)} %get-tuple-element.59.refs_1_), channel_id=1, source_target_pairs={{0,2},{1,3},{2,0},{3,1},{4,6},{5,7},{6,4},{7,5},{8,10},{9,11},{10,... | collective-permute-start | bytes 393224 | tf_op jit(solution)/shard_map/ppermute | solution.py:579
  29.5 2.1 %collective-permute-done.4.refs_1_.refs_0_.refs_6_ = bf16[144,1024]{1,0:T(8,128)(2,1)S(1)} collective-permute-done((bf16[144,1024]{1,0:T(8,128)(2,1)S(1)}, bf16[144,1024]{1,0:T(8,128)(2,1)S(1)}, u32[]{:S(2)}, u32[]{:S(2)}) %collective-permute-start.4) | collective-permute-done | bytes 294944 | tf_op jit(solution)/shard_map/ppermute | solution.py:579
  31.9 0.5 %project.12.refs_0_.refs_3_ = f32[128,1024]{1,0:T(8,128)S(1)} custom-call(bf16[1024,2048]{1,0:T(8,128)(2,1)S(1)} %after.2.refs_1_.refs_0_, bf16[128,1024]{1,0:T(8,128)(2,1)S(1)} %get-tuple-element.48.refs_1_.refs_3_), custom_call_target="tpu_custom_call" | custom-call | flops 1000000 | bytes 1024 | tf_op jit(solution)/shard_map/project/pallas_call | solution.py:364
  32.5 0.6 %collective-permute-done.6.refs_3_ = f32[1,256]{1,0:T(1,128)S(1)} collective-permute-done((f32[1,256]{1,0:T(1,128)S(1)}, f32[1,256]{1,0:T(1,128)S(1)}, u32[]{:S(2)}, u32[]{:S(2)}) %collective-permute-start.6) | collective-permute-done | bytes 1056 | tf_op jit(solution)/shard_map/ppermute | solution.py:579
  33.1 1.6 %collective-permute-start.9 = (bf16[144,1024]{1,0:T(8,128)(2,1)S(1)}, bf16[144,1024]{1,0:T(8,128)(2,1)S(1)}, u32[]{:S(2)}, u32[]{:S(2)}) collective-permute-start(bf16[144,1024]{1,0:T(8,128)(2,1)S(1)} %get-tuple-element.54), channel_id=1, source_target_pairs={{0,2},{1,3},{2,0},{3,1},{4,6},{5,7},{6,4},{7,5},{8,10},{9,11},{10,... | collective-permute-start | bytes 884744 | tf_op jit(solution)/shard_map/ppermute | solution.py:579
  34.7 1.3 %collective-permute-done.14.refs_3_ = bf16[128,512]{1,0:T(8,128)(2,1)S(1)} collective-permute-done((bf16[128,512]{1,0:T(8,128)(2,1)S(1)}, bf16[128,512]{1,0:T(8,128)(2,1)S(1)}, u32[]{:S(2)}, u32[]{:S(2)}) %collective-permute-start.14) | collective-permute-done | bytes 131104 | tf_op jit(solution)/shard_map/ppermute | solution.py:579
  36.0 1.6 %collective-permute-start.15 = (bf16[128,1024]{1,0:T(8,128)(2,1)S(1)}, bf16[128,1024]{1,0:T(8,128)(2,1)S(1)}, u32[]{:S(2)}, u32[]{:S(2)}) collective-permute-start(bf16[128,1024]{1,0:T(8,128)(2,1)S(1)} %merge.9), channel_id=1, source_target_pairs={{0,4},{1,5},{2,6},{3,7},{4,0},{5,1},{6,2},{7,3},{8,12},{9,13},{10,... | collective-permute-start | bytes 786440 | tf_op jit(solution)/shard_map/ppermute | solution.py:579
  37.6 4.7 %collective-permute-done.9.refs_7_.refs_5_ = bf16[144,1024]{1,0:T(8,128)(2,1)S(1)} collective-permute-done((bf16[144,1024]{1,0:T(8,128)(2,1)S(1)}, bf16[144,1024]{1,0:T(8,128)(2,1)S(1)}, u32[]{:S(2)}, u32[]{:S(2)}) %collective-permute-start.9) | collective-permute-done | bytes 294944 | tf_op jit(solution)/shard_map/ppermute | solution.py:579
  42.3 1.0 %finish.2 = (bf16[256,1024]{1,0:T(8,128)(2,1)}, f32[1,256]{1,0:T(1,128)}, f32[1,256]{1,0:T(1,128)S(1)}) custom-call(f32[1,256]{1,0:T(1,128)S(1)} %get-tuple-element.51.refs_0_, f32[1,128]{1,0:T(1,128)S(1)} %get-tuple-element.52.refs_1_, f32[1,1024]{1,0:T(1,128)S(1)} %get-tuple-element.53.refs_2_, f32[128,1024]{1,0:T(8,128)S(1)} %project.13.refs_0_.refs_3_, ...), custom_call_target="tpu_custom_call" | custom-call | flops 1000000 | bytes 1024 | tf_op jit(solution)/shard_map/finish/pallas_call | solution.py:546
  43.8 1.0 %finish.3 = bf16[256,1024]{1,0:T(8,128)(2,1)} custom-call(f32[1,256]{1,0:T(1,128)S(1)} %get-tuple-element.55.refs_0_, f32[1,128]{1,0:T(1,128)S(1)} %get-tuple-element.52.refs_1_, f32[1,1024]{1,0:T(1,128)S(1)} %get-tuple-element.53.refs_2_, f32[128,1024]{1,0:T(8,128)S(1)} %project.12.refs_0_.refs_3_, ...), custom_call_target="tpu_custom_call", output_to_operand_aliasing={{}: (7, {})} | custom-call | flops 1000000 | bytes 1024 | tf_op jit(solution)/shard_map/finish/pallas_call | solution.py:546
  (33 shorter events, 6.4 us)
Async XLA Ops:
  3.6 6.0 %collective-permute-start = (f32[176,128]{1,0:T(8,128)S(1)}, f32[176,128]{1,0:T(8,128)S(1)}, u32[]{:S(2)}, u32[]{:S(2)}) collective-permute-start(f32[176,128]{1,0:T(8,128)S(1)} %get-tuple-element.42), channel_id=1, source_target_pairs={{0,4},{1,5},{2,6},{3,7},{4,0},{5,1},{6,2},{7,3},{8,12},{9,13},{10,... | collective-permute-start | bytes 270344 | tf_op jit(solution)/shard_map/ppermute | solution.py:569
  10.8 4.0 %collective-permute-start.7 = (bf16[128,1024]{1,0:T(8,128)(2,1)S(1)}, bf16[128,1024]{1,0:T(8,128)(2,1)S(1)}, u32[]{:S(2)}, u32[]{:S(2)}) collective-permute-start(bf16[128,1024]{1,0:T(8,128)(2,1)S(1)} %project.8.refs_3_), channel_id=1, source_target_pairs={{0,1},{1,0},{2,3},{3,2},{4,5},{5,4},{6,7},{7,6},{8,9},{9,8},{10,11... | collective-permute-start | bytes 786440 | tf_op jit(solution)/shard_map/ppermute | solution.py:579
  10.9 9.2 %collective-permute-start.1 = (bf16[128,1024]{1,0:T(8,128)(2,1)S(1)}, bf16[128,1024]{1,0:T(8,128)(2,1)S(1)}, u32[]{:S(2)}, u32[]{:S(2)}) collective-permute-start(bf16[128,1024]{1,0:T(8,128)(2,1)S(1)} %get-tuple-element.44.refs_1_.refs_2_), channel_id=1, source_target_pairs={{0,4},{1,5},{2,6},{3,7},{4,0},{5,1},{6,2},{7,3},{8,12},{9,13},{10,... | collective-permute-start | bytes 786440 | tf_op jit(solution)/shard_map/ppermute | solution.py:575
  13.8 11.4 %collective-permute-start.10 = (bf16[128,1024]{1,0:T(8,128)(2,1)S(1)}, bf16[128,1024]{1,0:T(8,128)(2,1)S(1)}, u32[]{:S(2)}, u32[]{:S(2)}) collective-permute-start(bf16[128,1024]{1,0:T(8,128)(2,1)S(1)} %get-tuple-element.48.refs_1_.refs_3_), channel_id=1, source_target_pairs={{0,4},{1,5},{2,6},{3,7},{4,0},{5,1},{6,2},{7,3},{8,12},{9,13},{10,... | collective-permute-start | bytes 786440 | tf_op jit(solution)/shard_map/ppermute | solution.py:576
  14.9 10.4 %collective-permute-start.8 = (bf16[128,1024]{1,0:T(8,128)(2,1)S(1)}, bf16[128,1024]{1,0:T(8,128)(2,1)S(1)}, u32[]{:S(2)}, u32[]{:S(2)}) collective-permute-start(bf16[128,1024]{1,0:T(8,128)(2,1)S(1)} %merge.7), channel_id=1, source_target_pairs={{0,2},{1,3},{2,0},{3,1},{4,6},{5,7},{6,4},{7,5},{8,10},{9,11},{10,... | collective-permute-start | bytes 786440 | tf_op jit(solution)/shard_map/ppermute | solution.py:579
  20.6 1.4 %collective-permute-start.2 = (bf16[128,512]{1,0:T(8,128)(2,1)S(1)}, bf16[128,512]{1,0:T(8,128)(2,1)S(1)}, u32[]{:S(2)}, u32[]{:S(2)}) collective-permute-start(bf16[128,512]{1,0:T(8,128)(2,1)S(1)} %get-tuple-element.49), channel_id=1, source_target_pairs={{0,1},{1,0},{2,3},{3,2},{4,5},{5,4},{6,7},{7,6},{8,9},{9,8},{10,11... | collective-permute-start | bytes 393224 | tf_op jit(solution)/shard_map/ppermute | solution.py:579
  20.6 1.5 %collective-permute-start.3 = (bf16[128,512]{1,0:T(8,128)(2,1)S(1)}, bf16[128,512]{1,0:T(8,128)(2,1)S(1)}, u32[]{:S(2)}, u32[]{:S(2)}) collective-permute-start(bf16[128,512]{1,0:T(8,128)(2,1)S(1)} %get-tuple-element.50), channel_id=1, source_target_pairs={{0,1},{1,0},{2,3},{3,2},{4,5},{5,4},{6,7},{7,6},{8,9},{9,8},{10,11... | collective-permute-start | bytes 393224 | tf_op jit(solution)/shard_map/ppermute | solution.py:579
  22.2 9.3 %collective-permute-start.4 = (bf16[144,1024]{1,0:T(8,128)(2,1)S(1)}, bf16[144,1024]{1,0:T(8,128)(2,1)S(1)}, u32[]{:S(2)}, u32[]{:S(2)}) collective-permute-start(bf16[144,1024]{1,0:T(8,128)(2,1)S(1)} %merge.5.refs_1_), channel_id=1, source_target_pairs={{0,4},{1,5},{2,6},{3,7},{4,0},{5,1},{6,2},{7,3},{8,12},{9,13},{10,... | collective-permute-start | bytes 884744 | tf_op jit(solution)/shard_map/ppermute | solution.py:579
  23.8 8.6 %collective-permute-start.5 = (bf16[128,1024]{1,0:T(8,128)(2,1)S(1)}, bf16[128,1024]{1,0:T(8,128)(2,1)S(1)}, u32[]{:S(2)}, u32[]{:S(2)}) collective-permute-start(bf16[128,1024]{1,0:T(8,128)(2,1)S(1)} %project.9.refs_4_), channel_id=1, source_target_pairs={{0,1},{1,0},{2,3},{3,2},{4,5},{5,4},{6,7},{7,6},{8,9},{9,8},{10,11... | collective-permute-start | bytes 786440 | tf_op jit(solution)/shard_map/ppermute | solution.py:579
  25.7 1.4 %collective-permute-start.11 = (bf16[128,512]{1,0:T(8,128)(2,1)S(1)}, bf16[128,512]{1,0:T(8,128)(2,1)S(1)}, u32[]{:S(2)}, u32[]{:S(2)}) collective-permute-start(bf16[128,512]{1,0:T(8,128)(2,1)S(1)} %get-tuple-element.56), channel_id=1, source_target_pairs={{0,1},{1,0},{2,3},{3,2},{4,5},{5,4},{6,7},{7,6},{8,9},{9,8},{10,11... | collective-permute-start | bytes 393224 | tf_op jit(solution)/shard_map/ppermute | solution.py:579
  25.8 1.5 %collective-permute-start.12 = (bf16[128,512]{1,0:T(8,128)(2,1)S(1)}, bf16[128,512]{1,0:T(8,128)(2,1)S(1)}, u32[]{:S(2)}, u32[]{:S(2)}) collective-permute-start(bf16[128,512]{1,0:T(8,128)(2,1)S(1)} %get-tuple-element.57), channel_id=1, source_target_pairs={{0,1},{1,0},{2,3},{3,2},{4,5},{5,4},{6,7},{7,6},{8,9},{9,8},{10,11... | collective-permute-start | bytes 393224 | tf_op jit(solution)/shard_map/ppermute | solution.py:579
  27.4 7.3 %collective-permute-start.13 = (bf16[128,512]{1,0:T(8,128)(2,1)S(1)}, bf16[128,512]{1,0:T(8,128)(2,1)S(1)}, u32[]{:S(2)}, u32[]{:S(2)}) collective-permute-start(bf16[128,512]{1,0:T(8,128)(2,1)S(1)} %get-tuple-element.58.refs_0_), channel_id=1, source_target_pairs={{0,2},{1,3},{2,0},{3,1},{4,6},{5,7},{6,4},{7,5},{8,10},{9,11},{10,... | collective-permute-start | bytes 393224 | tf_op jit(solution)/shard_map/ppermute | solution.py:579
  28.9 7.0 %collective-permute-start.14 = (bf16[128,512]{1,0:T(8,128)(2,1)S(1)}, bf16[128,512]{1,0:T(8,128)(2,1)S(1)}, u32[]{:S(2)}, u32[]{:S(2)}) collective-permute-start(bf16[128,512]{1,0:T(8,128)(2,1)S(1)} %get-tuple-element.59.refs_1_), channel_id=1, source_target_pairs={{0,2},{1,3},{2,0},{3,1},{4,6},{5,7},{6,4},{7,5},{8,10},{9,11},{10,... | collective-permute-start | bytes 393224 | tf_op jit(solution)/shard_map/ppermute | solution.py:579
  31.9 1.2 %collective-permute-start.6 = (f32[1,256]{1,0:T(1,128)S(1)}, f32[1,256]{1,0:T(1,128)S(1)}, u32[]{:S(2)}, u32[]{:S(2)}) collective-permute-start(f32[1,256]{1,0:T(1,128)S(1)} %level.1.refs_2_), channel_id=1, source_target_pairs={{0,1},{1,0},{2,3},{3,2},{4,5},{5,4},{6,7},{7,6},{8,9},{9,8},{10,11... | collective-permute-start | bytes 3080 | tf_op jit(solution)/shard_map/ppermute | solution.py:579
  33.1 9.2 %collective-permute-start.9 = (bf16[144,1024]{1,0:T(8,128)(2,1)S(1)}, bf16[144,1024]{1,0:T(8,128)(2,1)S(1)}, u32[]{:S(2)}, u32[]{:S(2)}) collective-permute-start(bf16[144,1024]{1,0:T(8,128)(2,1)S(1)} %get-tuple-element.54), channel_id=1, source_target_pairs={{0,2},{1,3},{2,0},{3,1},{4,6},{5,7},{6,4},{7,5},{8,10},{9,11},{10,... | collective-permute-start | bytes 884744 | tf_op jit(solution)/shard_map/ppermute | solution.py:579
  36.0 7.8 %collective-permute-start.15 = (bf16[128,1024]{1,0:T(8,128)(2,1)S(1)}, bf16[128,1024]{1,0:T(8,128)(2,1)S(1)}, u32[]{:S(2)}, u32[]{:S(2)}) collective-permute-start(bf16[128,1024]{1,0:T(8,128)(2,1)S(1)} %merge.9), channel_id=1, source_target_pairs={{0,4},{1,5},{2,6},{3,7},{4,0},{5,1},{6,2},{7,3},{8,12},{9,13},{10,... | collective-permute-start | bytes 786440 | tf_op jit(solution)/shard_map/ppermute | solution.py:579

commit v2 on v1

--- a/solution.py
+++ b/solution.py
@@ -592,7 +592,7 @@
     (straight,) = exchange([sums0], across)
 
     sends, far_keep = run_project(weight, after(far_second, sums0, hop0), 0, rows - cut, 2)
-    sums1 = run_merge((far_keep,), exchange(sends, sibling), 2)
+    sums1 = run_merge((far_keep,), exchange(sends, sibling), 1)
     moved = exchange(sums1, pair)
     (core1,) = exchange(sends1, sibling)
     (own1,) = run_merge((keep1,), (core1,), 1)

time: 45 us -> 48.2 us (1.071)
  waiting for transfers between devices: 13.5 us -> 17.4 us
  starting transfers between devices: 14.8 us -> 14.1 us
    ppermute x13 -> x12, waiting for transfers between devices: 10.2 us -> 12.5 us  [exchange(): return [lax.ppermute(array, axes, pairs) for array in arrays]]
    ppermute x1, waiting for transfers between devices: 1.39 us -> 3.03 us  [plane_plan(): far_second = lax.ppermute(second, axes, across)]
    ppermute x13 -> x12, starting transfers between devices: 9.65 us -> 9 us  [exchange(): return [lax.ppermute(array, axes, pairs) for array in arrays]]
  transfers between devices with their start and end apart: 16 -> 15, of which waited for: 11 -> 7; matrix products, arithmetic and copies ran while one was open for 0% -> 0% of each run, Pallas kernels for 23% -> 21%
where the time goes in v2:
time: 48.2 us; the launch traced here: 48.1 us
  waiting for transfers between devices  17.4 us (36%)
  Pallas kernels  15.6 us (32%)
  starting transfers between devices  14.1 us (29%)
  between operations  0.85 us (2%)
    ppermute x12, waiting for transfers between devices, exchange(): return [lax.ppermute(array, axes, pairs) for array in arrays]  12.5 us
    ppermute x12, starting transfers between devices, exchange(): return [lax.ppermute(array, axes, pairs) for array in arrays]  9 us
    pallas_call x16, Pallas kernels, call(): pl.pallas_call(with_tokens, out_shape=out_shape, in_specs=[WHOLE] * len(o...  5.72 us
    ppermute x1, starting transfers between devices, plane_plan(): carry = lax.ppermute(ended, axes, across)  3.03 us
    ppermute x1, waiting for transfers between devices, plane_plan(): far_second = lax.ppermute(second, axes, across)  3.03 us
    pallas_call x1, Pallas kernels, run_front(): pl.pallas_call(front_kernel, out_shape=out_shape, in_specs=[AWAY] * 6, ou...  2.93 us
    pallas_call x1, Pallas kernels, run_local(): pl.pallas_call(local_kernel, out_shape=out_shape, in_specs=[WHOLE] * 5 +...  2.92 us
    pallas_call x2, Pallas kernels, run_correct(): pl.pallas_call(functools.partial(correct_kernel, blocks, start), out_shap...  2.04 us
  transfers between devices with their start and end apart: 15, of which 7 were waited for; matrix products, arithmetic and copies ran while one was open for 0% of the time, Pallas kernels for 21%

profile of v2, /device:TPU:0, one launch (start us, length us, event | category | flops | bytes accessed | tf_op | source)
XLA Modules:
  0.0 48.1 jit_solution(9836163700868362385)
XLA Ops:
  0.6 2.9 %front.1 = (f32[176,128]{1,0:T(8,128)S(1)}, f32[2048,128]{1,0:T(8,128)S(1)}, f32[128,128]{1,0:T(8,128)S(1)}, f32[72,128]{1,0:T(8,128)S(1)}, f32[32,128]{1,0:T(8,...) custom-call(bf16[256,1024]{1,0:T(8,128)(2,1)} %refs_0_.2, ...), custom_call_target="tpu_custom_call" | custom-call | flops 100000000 | bytes 1024 | tf_op jit(solution)/shard_map/front/pallas_call | solution.py:159
  3.6 3.0 %collective-permute-start = (f32[176,128]{1,0:T(8,128)S(1)}, f32[176,128]{1,0:T(8,128)S(1)}, u32[]{:S(2)}, u32[]{:S(2)}) collective-permute-start(f32[176,128]{1,0:T(8,128)S(1)} %get-tuple-element.40), channel_id=1, source_target_pairs={{0,4},{1,5},{2,6},{3,7},{4,0},{5,1},{6,2},{7,3},{8,12},{9,13},{10,... | collective-permute-start | bytes 270344 | tf_op jit(solution)/shard_map/ppermute | solution.py:569
  6.7 2.9 %local_filter.1 = (f32[2048,128]{1,0:T(8,128)S(1)}, f32[2048,128]{1,0:T(8,128)S(1)}, f32[128,128]{1,0:T(8,128)S(1)}, bf16[1024,2048]{1,0:T(8,128)(2,1)S(1)}, f32[1,4096]{1,0:T(1,128)S(1)}) custom-call(bf16[256,1024]{1,0:T(8,128)(2,1)S(1)} %get-tuple-element.30.q_near, f32[2048,128]{1,0:T(8,128)S(1)} %get-tuple-element.31.signal_ref, ...), custom_call_target="tpu_custom_call" | custom-call | flops 1000000 | bytes 1024 | tf_op jit(solution)/shard_map/local_filter/pallas_call | solution.py:235
  9.6 0.7 %carried_filter.2 = (bf16[128,1024]{1,0:T(8,128)(2,1)S(1)}, f32[128,128]{1,0:T(8,128)S(1)}) custom-call(f32[128,128]{1,0:T(8,128)S(1)} %get-tuple-element.32.decay_ref, f32[128,128]{1,0:T(8,128)S(1)} %get-tuple-element.37.gain_ref, f32[2048,128]{1,0:T(8,128)S(1)} %get-tuple-element.38.local_ref, f32[2048,128]{1,0:T(8,128)S(1)} %get-tuple-element.39.query_ref, ...), custom_call_target="tpu_custom_call" | custom-call | flops 100000000 | bytes 1024 | tf_op jit(solution)/shard_map/carried_filter/pallas_call | solution.py:303
  10.3 0.5 %project.8.refs_3_ = bf16[128,1024]{1,0:T(8,128)(2,1)S(1)} custom-call(bf16[1024,2048]{1,0:T(8,128)(2,1)S(1)} %after.2.refs_1_.refs_0_, bf16[128,1024]{1,0:T(8,128)(2,1)S(1)} %get-tuple-element.42.refs_1_.refs_2_), custom_call_target="tpu_custom_call" | custom-call | flops 1000000 | bytes 1024 | tf_op jit(solution)/shard_map/project/pallas_call | solution.py:364
  10.9 1.6 %collective-permute-start.1 = (bf16[128,1024]{1,0:T(8,128)(2,1)S(1)}, bf16[128,1024]{1,0:T(8,128)(2,1)S(1)}, u32[]{:S(2)}, u32[]{:S(2)}) collective-permute-start(bf16[128,1024]{1,0:T(8,128)(2,1)S(1)} %get-tuple-element.42.refs_1_.refs_2_), channel_id=1, source_target_pairs={{0,4},{1,5},{2,6},{3,7},{4,0},{5,1},{6,2},{7,3},{8,12},{9,13},{10,... | collective-permute-start | bytes 786440 | tf_op jit(solution)/shard_map/ppermute | solution.py:575
  12.5 1.3 %carried_filter.3 = (bf16[128,1024]{1,0:T(8,128)(2,1)S(1)}, f32[128,128]{1,0:T(8,128)}) custom-call(f32[128,128]{1,0:T(8,128)S(1)} %get-tuple-element.32.decay_ref, f32[128,128]{1,0:T(8,128)S(1)} %get-tuple-element.37.gain_ref, f32[2048,128]{1,0:T(8,128)S(1)} %get-tuple-element.38.local_ref, f32[2048,128]{1,0:T(8,128)S(1)} %get-tuple-element.39.query_ref, ...), custom_call_target="tpu_custom_call" | custom-call | flops 100000000 | bytes 1024 | tf_op jit(solution)/shard_map/carried_filter/pallas_call | solution.py:303
  13.8 0.5 %collective-permute-start.10 = (bf16[128,1024]{1,0:T(8,128)(2,1)S(1)}, bf16[128,1024]{1,0:T(8,128)(2,1)S(1)}, u32[]{:S(2)}, u32[]{:S(2)}) collective-permute-start(bf16[128,1024]{1,0:T(8,128)(2,1)S(1)} %get-tuple-element.46.refs_1_.refs_3_), channel_id=1, source_target_pairs={{0,4},{1,5},{2,6},{3,7},{4,0},{5,1},{6,2},{7,3},{8,12},{9,13},{10,... | collective-permute-start | bytes 786440 | tf_op jit(solution)/shard_map/ppermute | solution.py:576
  14.9 1.6 %collective-permute-start.8 = (bf16[128,1024]{1,0:T(8,128)(2,1)S(1)}, bf16[128,1024]{1,0:T(8,128)(2,1)S(1)}, u32[]{:S(2)}, u32[]{:S(2)}) collective-permute-start(bf16[128,1024]{1,0:T(8,128)(2,1)S(1)} %merge.7), channel_id=1, source_target_pairs={{0,2},{1,3},{2,0},{3,1},{4,6},{5,7},{6,4},{7,5},{8,10},{9,11},{10,... | collective-permute-start | bytes 786440 | tf_op jit(solution)/shard_map/ppermute | solution.py:579
  16.9 1.2 %inner.1 = (bf16[16,1024]{1,0:T(8,128)(2,1)S(1)}, f32[1,128]{1,0:T(1,128)S(1)}, f32[1,1024]{1,0:T(1,128)S(1)}) custom-call(f32[1,4096]{1,0:T(1,128)S(1)} %get-tuple-element.43.refs_0_, bf16[1024,2048]{1,0:T(8,128)(2,1)S(1)} %after.2.refs_1_.refs_0_), custom_call_target="tpu_custom_call" | custom-call | flops 1000000 | bytes 1024 | tf_op jit(solution)/shard_map/inner/pallas_call | solution.py:364
  18.1 1.9 %collective-permute-done.1.refs_1_ = bf16[128,1024]{1,0:T(8,128)(2,1)S(1)} collective-permute-done((bf16[128,1024]{1,0:T(8,128)(2,1)S(1)}, bf16[128,1024]{1,0:T(8,128)(2,1)S(1)}, u32[]{:S(2)}, u32[]{:S(2)}) %collective-permute-start.1) | collective-permute-done | bytes 262176 | tf_op jit(solution)/shard_map/ppermute | solution.py:575
  20.6 0.5 %collective-permute-start.3 = (bf16[128,512]{1,0:T(8,128)(2,1)S(1)}, bf16[128,512]{1,0:T(8,128)(2,1)S(1)}, u32[]{:S(2)}, u32[]{:S(2)}) collective-permute-start(bf16[128,512]{1,0:T(8,128)(2,1)S(1)} %get-tuple-element.48), channel_id=1, source_target_pairs={{0,1},{1,0},{2,3},{3,2},{4,5},{5,4},{6,7},{7,6},{8,9},{9,8},{10,11... | collective-permute-start | bytes 393224 | tf_op jit(solution)/shard_map/ppermute | solution.py:579
  22.2 3.0 %collective-permute-done.10.refs_0_ = bf16[128,1024]{1,0:T(8,128)(2,1)S(1)} collective-permute-done((bf16[128,1024]{1,0:T(8,128)(2,1)S(1)}, bf16[128,1024]{1,0:T(8,128)(2,1)S(1)}, u32[]{:S(2)}, u32[]{:S(2)}) %collective-permute-start.10) | collective-permute-done | bytes 262176 | tf_op jit(solution)/shard_map/ppermute | solution.py:576
  25.8 0.5 %collective-permute-start.12 = (bf16[128,512]{1,0:T(8,128)(2,1)S(1)}, bf16[128,512]{1,0:T(8,128)(2,1)S(1)}, u32[]{:S(2)}, u32[]{:S(2)}) collective-permute-start(bf16[128,512]{1,0:T(8,128)(2,1)S(1)} %get-tuple-element.55), channel_id=1, source_target_pairs={{0,1},{1,0},{2,3},{3,2},{4,5},{5,4},{6,7},{7,6},{8,9},{9,8},{10,11... | collective-permute-start | bytes 393224 | tf_op jit(solution)/shard_map/ppermute | solution.py:579
  26.3 1.5 %collective-permute-start.4 = (bf16[144,1024]{1,0:T(8,128)(2,1)S(1)}, bf16[144,1024]{1,0:T(8,128)(2,1)S(1)}, u32[]{:S(2)}, u32[]{:S(2)}) collective-permute-start(bf16[144,1024]{1,0:T(8,128)(2,1)S(1)} %merge.5.refs_1_), channel_id=1, source_target_pairs={{0,4},{1,5},{2,6},{3,7},{4,0},{5,1},{6,2},{7,3},{8,12},{9,13},{10,... | collective-permute-start | bytes 884744 | tf_op jit(solution)/shard_map/ppermute | solution.py:579
  28.4 1.6 %collective-permute-start.13 = (bf16[128,1024]{1,0:T(8,128)(2,1)S(1)}, bf16[128,1024]{1,0:T(8,128)(2,1)S(1)}, u32[]{:S(2)}, u32[]{:S(2)}) collective-permute-start(bf16[128,1024]{1,0:T(8,128)(2,1)S(1)} %merge.8.refs_0_), channel_id=1, source_target_pairs={{0,2},{1,3},{2,0},{3,1},{4,6},{5,7},{6,4},{7,5},{8,10},{9,11},{10,... | collective-permute-start | bytes 786440 | tf_op jit(solution)/shard_map/ppermute | solution.py:579
  29.9 5.4 %collective-permute-done.4.refs_1_.refs_0_.refs_6_ = bf16[144,1024]{1,0:T(8,128)(2,1)S(1)} collective-permute-done((bf16[144,1024]{1,0:T(8,128)(2,1)S(1)}, bf16[144,1024]{1,0:T(8,128)(2,1)S(1)}, u32[]{:S(2)}, u32[]{:S(2)}) %collective-permute-start.4) | collective-permute-done | bytes 294944 | tf_op jit(solution)/shard_map/ppermute | solution.py:579
  35.7 0.5 %project.12.refs_0_.refs_3_ = f32[128,1024]{1,0:T(8,128)S(1)} custom-call(bf16[1024,2048]{1,0:T(8,128)(2,1)S(1)} %after.2.refs_1_.refs_0_, bf16[128,1024]{1,0:T(8,128)(2,1)S(1)} %get-tuple-element.46.refs_1_.refs_3_), custom_call_target="tpu_custom_call" | custom-call | flops 1000000 | bytes 1024 | tf_op jit(solution)/shard_map/project/pallas_call | solution.py:364
  36.2 0.6 %collective-permute-done.6.refs_3_ = f32[1,256]{1,0:T(1,128)S(1)} collective-permute-done((f32[1,256]{1,0:T(1,128)S(1)}, f32[1,256]{1,0:T(1,128)S(1)}, u32[]{:S(2)}, u32[]{:S(2)}) %collective-permute-start.6) | collective-permute-done | bytes 1056 | tf_op jit(solution)/shard_map/ppermute | solution.py:579
  36.9 1.6 %collective-permute-start.9 = (bf16[144,1024]{1,0:T(8,128)(2,1)S(1)}, bf16[144,1024]{1,0:T(8,128)(2,1)S(1)}, u32[]{:S(2)}, u32[]{:S(2)}) collective-permute-start(bf16[144,1024]{1,0:T(8,128)(2,1)S(1)} %get-tuple-element.52), channel_id=1, source_target_pairs={{0,2},{1,3},{2,0},{3,1},{4,6},{5,7},{6,4},{7,5},{8,10},{9,11},{10,... | collective-permute-start | bytes 884744 | tf_op jit(solution)/shard_map/ppermute | solution.py:579
  38.5 1.6 %collective-permute-start.14 = (bf16[128,1024]{1,0:T(8,128)(2,1)S(1)}, bf16[128,1024]{1,0:T(8,128)(2,1)S(1)}, u32[]{:S(2)}, u32[]{:S(2)}) collective-permute-start(bf16[128,1024]{1,0:T(8,128)(2,1)S(1)} %merge.9), channel_id=1, source_target_pairs={{0,4},{1,5},{2,6},{3,7},{4,0},{5,1},{6,2},{7,3},{8,12},{9,13},{10,... | collective-permute-start | bytes 786440 | tf_op jit(solution)/shard_map/ppermute | solution.py:579
  40.1 6.0 %collective-permute-done.9.refs_7_.refs_5_ = bf16[144,1024]{1,0:T(8,128)(2,1)S(1)} collective-permute-done((bf16[144,1024]{1,0:T(8,128)(2,1)S(1)}, bf16[144,1024]{1,0:T(8,128)(2,1)S(1)}, u32[]{:S(2)}, u32[]{:S(2)}) %collective-permute-start.9) | collective-permute-done | bytes 294944 | tf_op jit(solution)/shard_map/ppermute | solution.py:579
  46.0 1.0 %finish.2 = (bf16[256,1024]{1,0:T(8,128)(2,1)}, f32[1,256]{1,0:T(1,128)}, f32[1,256]{1,0:T(1,128)S(1)}) custom-call(f32[1,256]{1,0:T(1,128)S(1)} %get-tuple-element.49.refs_0_, f32[1,128]{1,0:T(1,128)S(1)} %get-tuple-element.50.refs_1_, f32[1,1024]{1,0:T(1,128)S(1)} %get-tuple-element.51.refs_2_, f32[128,1024]{1,0:T(8,128)S(1)} %project.13.refs_0_.refs_3_, ...), custom_call_target="tpu_custom_call" | custom-call | flops 1000000 | bytes 1024 | tf_op jit(solution)/shard_map/finish/pallas_call | solution.py:546
  47.1 1.0 %finish.3 = bf16[256,1024]{1,0:T(8,128)(2,1)} custom-call(f32[1,256]{1,0:T(1,128)S(1)} %get-tuple-element.53.refs_0_, f32[1,128]{1,0:T(1,128)S(1)} %get-tuple-element.50.refs_1_, f32[1,1024]{1,0:T(1,128)S(1)} %get-tuple-element.51.refs_2_, f32[128,1024]{1,0:T(8,128)S(1)} %project.12.refs_0_.refs_3_, ...), custom_call_target="tpu_custom_call", output_to_operand_aliasing={{}: (7, {})} | custom-call | flops 1000000 | bytes 1024 | tf_op jit(solution)/shard_map/finish/pallas_call | solution.py:546
  (31 shorter events, 4.3 us)
Async XLA Ops:
  3.6 6.0 %collective-permute-start = (f32[176,128]{1,0:T(8,128)S(1)}, f32[176,128]{1,0:T(8,128)S(1)}, u32[]{:S(2)}, u32[]{:S(2)}) collective-permute-start(f32[176,128]{1,0:T(8,128)S(1)} %get-tuple-element.40), channel_id=1, source_target_pairs={{0,4},{1,5},{2,6},{3,7},{4,0},{5,1},{6,2},{7,3},{8,12},{9,13},{10,... | collective-permute-start | bytes 270344 | tf_op jit(solution)/shard_map/ppermute | solution.py:569
  10.8 4.0 %collective-permute-start.7 = (bf16[128,1024]{1,0:T(8,128)(2,1)S(1)}, bf16[128,1024]{1,0:T(8,128)(2,1)S(1)}, u32[]{:S(2)}, u32[]{:S(2)}) collective-permute-start(bf16[128,1024]{1,0:T(8,128)(2,1)S(1)} %project.8.refs_3_), channel_id=1, source_target_pairs={{0,1},{1,0},{2,3},{3,2},{4,5},{5,4},{6,7},{7,6},{8,9},{9,8},{10,11... | collective-permute-start | bytes 786440 | tf_op jit(solution)/shard_map/ppermute | solution.py:579
  10.9 9.2 %collective-permute-start.1 = (bf16[128,1024]{1,0:T(8,128)(2,1)S(1)}, bf16[128,1024]{1,0:T(8,128)(2,1)S(1)}, u32[]{:S(2)}, u32[]{:S(2)}) collective-permute-start(bf16[128,1024]{1,0:T(8,128)(2,1)S(1)} %get-tuple-element.42.refs_1_.refs_2_), channel_id=1, source_target_pairs={{0,4},{1,5},{2,6},{3,7},{4,0},{5,1},{6,2},{7,3},{8,12},{9,13},{10,... | collective-permute-start | bytes 786440 | tf_op jit(solution)/shard_map/ppermute | solution.py:575
  13.8 11.4 %collective-permute-start.10 = (bf16[128,1024]{1,0:T(8,128)(2,1)S(1)}, bf16[128,1024]{1,0:T(8,128)(2,1)S(1)}, u32[]{:S(2)}, u32[]{:S(2)}) collective-permute-start(bf16[128,1024]{1,0:T(8,128)(2,1)S(1)} %get-tuple-element.46.refs_1_.refs_3_), channel_id=1, source_target_pairs={{0,4},{1,5},{2,6},{3,7},{4,0},{5,1},{6,2},{7,3},{8,12},{9,13},{10,... | collective-permute-start | bytes 786440 | tf_op jit(solution)/shard_map/ppermute | solution.py:576
  14.9 10.4 %collective-permute-start.8 = (bf16[128,1024]{1,0:T(8,128)(2,1)S(1)}, bf16[128,1024]{1,0:T(8,128)(2,1)S(1)}, u32[]{:S(2)}, u32[]{:S(2)}) collective-permute-start(bf16[128,1024]{1,0:T(8,128)(2,1)S(1)} %merge.7), channel_id=1, source_target_pairs={{0,2},{1,3},{2,0},{3,1},{4,6},{5,7},{6,4},{7,5},{8,10},{9,11},{10,... | collective-permute-start | bytes 786440 | tf_op jit(solution)/shard_map/ppermute | solution.py:579
  20.6 1.4 %collective-permute-start.2 = (bf16[128,512]{1,0:T(8,128)(2,1)S(1)}, bf16[128,512]{1,0:T(8,128)(2,1)S(1)}, u32[]{:S(2)}, u32[]{:S(2)}) collective-permute-start(bf16[128,512]{1,0:T(8,128)(2,1)S(1)} %get-tuple-element.47), channel_id=1, source_target_pairs={{0,1},{1,0},{2,3},{3,2},{4,5},{5,4},{6,7},{7,6},{8,9},{9,8},{10,11... | collective-permute-start | bytes 393224 | tf_op jit(solution)/shard_map/ppermute | solution.py:579
  20.6 1.5 %collective-permute-start.3 = (bf16[128,512]{1,0:T(8,128)(2,1)S(1)}, bf16[128,512]{1,0:T(8,128)(2,1)S(1)}, u32[]{:S(2)}, u32[]{:S(2)}) collective-permute-start(bf16[128,512]{1,0:T(8,128)(2,1)S(1)} %get-tuple-element.48), channel_id=1, source_target_pairs={{0,1},{1,0},{2,3},{3,2},{4,5},{5,4},{6,7},{7,6},{8,9},{9,8},{10,11... | collective-permute-start | bytes 393224 | tf_op jit(solution)/shard_map/ppermute | solution.py:579
  25.7 2.6 %collective-permute-start.11 = (bf16[128,512]{1,0:T(8,128)(2,1)S(1)}, bf16[128,512]{1,0:T(8,128)(2,1)S(1)}, u32[]{:S(2)}, u32[]{:S(2)}) collective-permute-start(bf16[128,512]{1,0:T(8,128)(2,1)S(1)} %get-tuple-element.54), channel_id=1, source_target_pairs={{0,1},{1,0},{2,3},{3,2},{4,5},{5,4},{6,7},{7,6},{8,9},{9,8},{10,11... | collective-permute-start | bytes 393224 | tf_op jit(solution)/shard_map/ppermute | solution.py:579
  25.8 2.5 %collective-permute-start.12 = (bf16[128,512]{1,0:T(8,128)(2,1)S(1)}, bf16[128,512]{1,0:T(8,128)(2,1)S(1)}, u32[]{:S(2)}, u32[]{:S(2)}) collective-permute-start(bf16[128,512]{1,0:T(8,128)(2,1)S(1)} %get-tuple-element.55), channel_id=1, source_target_pairs={{0,1},{1,0},{2,3},{3,2},{4,5},{5,4},{6,7},{7,6},{8,9},{9,8},{10,11... | collective-permute-start | bytes 393224 | tf_op jit(solution)/shard_map/ppermute | solution.py:579
  26.3 9.0 %collective-permute-start.4 = (bf16[144,1024]{1,0:T(8,128)(2,1)S(1)}, bf16[144,1024]{1,0:T(8,128)(2,1)S(1)}, u32[]{:S(2)}, u32[]{:S(2)}) collective-permute-start(bf16[144,1024]{1,0:T(8,128)(2,1)S(1)} %merge.5.refs_1_), channel_id=1, source_target_pairs={{0,4},{1,5},{2,6},{3,7},{4,0},{5,1},{6,2},{7,3},{8,12},{9,13},{10,... | collective-permute-start | bytes 884744 | tf_op jit(solution)/shard_map/ppermute | solution.py:579
  27.8 8.3 %collective-permute-start.5 = (bf16[128,1024]{1,0:T(8,128)(2,1)S(1)}, bf16[128,1024]{1,0:T(8,128)(2,1)S(1)}, u32[]{:S(2)}, u32[]{:S(2)}) collective-permute-start(bf16[128,1024]{1,0:T(8,128)(2,1)S(1)} %project.9.refs_4_), channel_id=1, source_target_pairs={{0,1},{1,0},{2,3},{3,2},{4,5},{5,4},{6,7},{7,6},{8,9},{9,8},{10,11... | collective-permute-start | bytes 786440 | tf_op jit(solution)/shard_map/ppermute | solution.py:579
  28.4 10.0 %collective-permute-start.13 = (bf16[128,1024]{1,0:T(8,128)(2,1)S(1)}, bf16[128,1024]{1,0:T(8,128)(2,1)S(1)}, u32[]{:S(2)}, u32[]{:S(2)}) collective-permute-start(bf16[128,1024]{1,0:T(8,128)(2,1)S(1)} %merge.8.refs_0_), channel_id=1, source_target_pairs={{0,2},{1,3},{2,0},{3,1},{4,6},{5,7},{6,4},{7,5},{8,10},{9,11},{10,... | collective-permute-start | bytes 786440 | tf_op jit(solution)/shard_map/ppermute | solution.py:579
  35.7 1.2 %collective-permute-start.6 = (f32[1,256]{1,0:T(1,128)S(1)}, f32[1,256]{1,0:T(1,128)S(1)}, u32[]{:S(2)}, u32[]{:S(2)}) collective-permute-start(f32[1,256]{1,0:T(1,128)S(1)} %level.1.refs_2_), channel_id=1, source_target_pairs={{0,1},{1,0},{2,3},{3,2},{4,5},{5,4},{6,7},{7,6},{8,9},{9,8},{10,11... | collective-permute-start | bytes 3080 | tf_op jit(solution)/shard_map/ppermute | solution.py:579
  36.9 9.2 %collective-permute-start.9 = (bf16[144,1024]{1,0:T(8,128)(2,1)S(1)}, bf16[144,1024]{1,0:T(8,128)(2,1)S(1)}, u32[]{:S(2)}, u32[]{:S(2)}) collective-permute-start(bf16[144,1024]{1,0:T(8,128)(2,1)S(1)} %get-tuple-element.52), channel_id=1, source_target_pairs={{0,2},{1,3},{2,0},{3,1},{4,6},{5,7},{6,4},{7,5},{8,10},{9,11},{10,... | collective-permute-start | bytes 884744 | tf_op jit(solution)/shard_map/ppermute | solution.py:579
  38.5 8.6 %collective-permute-start.14 = (bf16[128,1024]{1,0:T(8,128)(2,1)S(1)}, bf16[128,1024]{1,0:T(8,128)(2,1)S(1)}, u32[]{:S(2)}, u32[]{:S(2)}) collective-permute-start(bf16[128,1024]{1,0:T(8,128)(2,1)S(1)} %merge.9), channel_id=1, source_target_pairs={{0,4},{1,5},{2,6},{3,7},{4,0},{5,1},{6,2},{7,3},{8,12},{9,13},{10,... | collective-permute-start | bytes 786440 | tf_op jit(solution)/shard_map/ppermute | solution.py:579
